TPU v7x, 512 devices: a whole 4x4x16 slice. The times are simulated.
512 devices in a mesh: grp: 32 (over z, core), tp: 16 (over x, y).
Axes of the slice: x: 4, y: 4, z: 16, core: 2. Of those that a mesh axis runs over, the one named last changes fastest.
Arguments:
- query_nope: bfloat16 [8192, 8192], P('grp', 'tp'), may hold values from -6 to 6
- query_rope: bfloat16 [8192, 4096], P('grp', 'tp'), may hold values from -24 to 24
- latent_cache: bfloat16 [65536, 576], P('grp'), may hold values from -6 to 6
- new_latent: bfloat16 [64, 128, 576], P('grp', 'tp'), may hold values from -6 to 6
- prefix_length: int32 [32], P('grp'), may hold values from 2 to 2048, as said below
- latent_up: bfloat16 [512, 16384], P(None, 'tp'), may hold values from -0.5 to 0.5
- out_proj: bfloat16 [8192, 4096], P('tp', 'grp'), may hold values from -0.25 to 0.25
- owners: int32 [64], replicated, may hold values from 0 to 31, as said below
- slot_index: int32 [64], replicated, may hold values from 0 to 3, as said below
Outputs:
- mixed: bfloat16 [8192, 4096], P(('grp', 'tp'))
- decode_cache: bfloat16 [128, 128, 576], P('grp', 'tp')
Inputs may be any that keep to these rules, and one draw needn't show every extreme that they name: `prefix_length`: some group uses all 2048 cached positions. Each owner receives at most 4 blocks, and some owner receives exactly 4; the 2 blocks of one group have different owners. `slot_index`: blocks of one owner have different slots.
All inputs are finite; a program needn't handle non-finite values.
Results may differ from a plain program's by a relative error of at most 0.018.
Values may be sent and summed in bfloat16 or wider, within the bound.
A program may use at most 64 MiB of HBM per device.

v0:
```python
import jax
import jax.numpy as jnp
from jax import lax
from jax.sharding import PartitionSpec as P

NOPE = 128
ROPE = 64
VDIM = 128
KVR = 512
SLOTS = 4


def attend_heads(query_nope, query_rope, key_rows, length, latent_up):
    span = query_nope.shape[0]
    total = key_rows.shape[0]
    prefix = total - span
    heads_dev = query_nope.shape[1] // NOPE
    score_scale = (NOPE + ROPE) ** (-0.5)
    row_ids = jnp.arange(span, dtype=jnp.int32)[:, None]
    col_ids = jnp.arange(total, dtype=jnp.int32)[None, :]
    visible = jnp.where(col_ids < prefix, col_ids < length, col_ids - prefix <= row_ids)
    up_heads = latent_up.reshape(KVR, heads_dev, NOPE + VDIM)
    absorbed = jnp.einsum(
        "chd,khd->hck",
        query_nope.reshape(span, heads_dev, NOPE),
        up_heads[:, :, :NOPE],
        preferred_element_type=jnp.float32,
    ).astype(jnp.bfloat16)
    rotary = query_rope.reshape(span, heads_dev, ROPE).transpose(1, 0, 2)
    queries = jnp.concatenate([absorbed, rotary], axis=2).reshape(heads_dev * span, KVR + ROPE)
    scores = (
        lax.dot_general(
            queries, key_rows, (((1,), (1,)), ((), ())), preferred_element_type=jnp.float32
        )
        * score_scale
    )
    scores = jnp.where(visible[None], scores.reshape(heads_dev, span, total), -jnp.inf)
    highest = jnp.max(scores, axis=2, keepdims=True)
    expo = jnp.exp(scores - highest)
    soft_weights = (expo / jnp.sum(expo, axis=2, keepdims=True)).astype(jnp.bfloat16)
    latent_out = jnp.dot(
        soft_weights.reshape(heads_dev * span, total),
        key_rows[:, :KVR],
        preferred_element_type=jnp.float32,
    ).astype(jnp.bfloat16)
    latent_out = latent_out.reshape(heads_dev, span, KVR)
    values = jnp.einsum(
        "hck,khd->chd", latent_out, up_heads[:, :, NOPE:], preferred_element_type=jnp.float32
    )
    return values.astype(jnp.bfloat16).reshape(span, heads_dev * VDIM)


def body(
    query_nope,
    query_rope,
    latent_cache,
    new_latent,
    prefix_length,
    latent_up,
    out_proj,
    owners,
    slot_index,
):
    grp_count = lax.axis_size("grp")
    span = query_nope.shape[0]
    width = latent_cache.shape[1]
    fresh = lax.all_gather(new_latent, "tp", axis=1, tiled=True).reshape(span, width)
    key_rows = jnp.concatenate([latent_cache, fresh], axis=0)
    attended = attend_heads(query_nope, query_rope, key_rows, prefix_length[0], latent_up)
    partial_value = jnp.dot(
        attended,
        lax.all_gather(out_proj, "grp", axis=1, tiled=True),
        preferred_element_type=jnp.float32,
    )
    mixed = lax.psum_scatter(
        partial_value.astype(jnp.bfloat16), "tp", scatter_dimension=0, tiled=True
    )
    rank_here = lax.axis_index("grp")
    blocks_dev = new_latent.shape[0]
    block_rows = new_latent.shape[1]
    targets = jnp.arange(SLOTS, dtype=jnp.int32)
    own_owner = lax.dynamic_slice_in_dim(owners, rank_here * blocks_dev, blocks_dev)
    destinations = jnp.arange(grp_count, dtype=jnp.int32)
    routing = (destinations[:, None] == own_owner[None, :]).astype(jnp.bfloat16)
    outgoing = jnp.dot(
        routing,
        new_latent.reshape(blocks_dev, block_rows * width),
        preferred_element_type=jnp.float32,
    ).astype(jnp.bfloat16)
    received = lax.all_to_all(outgoing, "grp", split_axis=0, concat_axis=0, tiled=True)
    owner_grid = owners.reshape(grp_count, blocks_dev)
    slot_grid = slot_index.reshape(grp_count, blocks_dev)
    hits = (owner_grid[None, :, :] == rank_here) & (slot_grid[None, :, :] == targets[:, None, None])
    selector = jnp.sum(hits.astype(jnp.float32), axis=2).astype(jnp.bfloat16)
    picked = jnp.dot(selector, received, preferred_element_type=jnp.float32)
    decode_cache = picked.astype(jnp.bfloat16).reshape(SLOTS, block_rows, width)
    return (mixed, decode_cache)


def solution(mesh):
    placed = (
        P("grp", "tp"),
        P("grp", "tp"),
        P("grp", None),
        P("grp", "tp", None),
        P("grp"),
        P(None, "tp"),
        P("tp", "grp"),
        P(),
        P(),
    )
    return jax.shard_map(
        body,
        mesh=mesh,
        in_specs=placed,
        out_specs=(P(("grp", "tp"), None), P("grp", "tp", None)),
        check_vma=False,
    )
```

profile of v0, /device:TPU:1, one launch (start us, length us, event | category | flops | bytes accessed | tf_op | source)
XLA Modules:
  0.0 191.8 jit_solution(5658597177793107060)
XLA Ops:
  7.2 0.7 all-gather.2.cloned.1.call-update
  8.6 2.4 %copy.34 = bf16[512,1024]{0,1:T(8,128)(2,1)} copy(bf16[512,1024]{1,0:T(8,128)(2,1)} %param.14) | data formatting | bytes 2097152 | tf_op args[5]
  11.1 1.0 copy.37
  12.1 0.2 copy.38
  12.2 19.9 %all_gather.6 = bf16[2,128,576]{2,1,0:T(8,128)(2,1)S(1)} all-gather(bf16[2,8,576]{2,1,0:T(8,128)(2,1)} %param.12), channel_id=1, replica_groups=mesh['grp'=32,'tp'=16] {'tp'}, dimensions={1}, use_global_device_ids=true | all-gather | bytes 313344 | tf_op jit(solution)/shard_map/all_gather | solution.py:67
  32.2 0.2 copy.39
  32.4 1.5 convolution_convert_fusion.3
  33.8 0.1 pad_maximum_fusion
  33.9 0.4 fusion.11
  34.4 4.5 %fusion = (f32[1024]{0:T(1024)S(1)}, f32[1024,2304]{1,0:T(8,128)S(1)}) fusion(pred[256,2304]{1,0:T(8,128)(4,1)S(1)} %fusion.11, bf16[1024,576]{1,0:T(8,128)(2,1)S(1)} %bitcast.40, bf16[256,576]{0,1:T(8,128)(2,1)S(1)} %copy.39, bf16[2048,576]{0,1:T(8,128)(2,1)S(1)} %copy-done.1), kind=kOutput, calls=%fused_computation.3 | convolution fusion | flops 2730294272 | bytes 13864960 | tf_op jit(solution)/shard_map/dot_general | solution.py:32
  38.8 2.8 %fusion.1 = f32[1024]{0:T(1024)S(1)} fusion(f32[1024,2304]{1,0:T(8,128)S(1)} %get-tuple-element.3, f32[1024]{0:T(1024)S(1)} %get-tuple-element.2, pred[256,2304]{1,0:T(8,128)(4,1)S(1)} %fusion.11), kind=kLoop, calls=%fused_computation.4 | loop fusion | flops 9436160 | bytes 10035200 | tf_op jit(solution)/shard_map/reduce_sum | solution.py:40
  41.6 3.4 %divide_convert_fusion = bf16[1024,2304]{1,0:T(8,128)(2,1)S(1)} fusion(f32[1024,2304]{1,0:T(8,128)S(1)} %get-tuple-element.3, f32[1024]{0:T(1024)S(1)} %fusion.1, f32[1024]{0:T(1024)S(1)} %get-tuple-element.2, pred[256,2304]{1,0:T(8,128)(4,1)S(1)} %fusion.11), kind=kLoop, calls=%fused_computation | loop fusion | flops 11796480 | bytes 14753792 | tf_op jit(solution)/shard_map/convert_element_type | solution.py:40
  45.0 2.6 %fusion.12 = bf16[1024,512]{1,0:T(8,128)(2,1)S(1)} fusion(bf16[1024,2304]{1,0:T(8,128)(2,1)S(1)} %divide_convert_fusion, bf16[256,576]{0,1:T(8,128)(2,1)S(1)} %copy.39, bf16[2048,576]{0,1:T(8,128)(2,1)S(1)} %copy-done.1), kind=kOutput, calls=%fused_computation.19 | convolution fusion | flops 2421161984 | bytes 8421376 | tf_op jit(solution)/shard_map/dot_general | solution.py:41
  47.7 0.5 convolution_convert_fusion.4
  48.2 47.7 %all-gather.2.cloned.1.call-done = bf16[512,4096]{1,0:T(8,128)(2,1)} async-done(((bf16[512,128]{1,0:T(8,128)(2,1)}), bf16[512,4096]{1,0:T(8,128)(2,1)}) %all-gather.2.cloned.1.call-update) | async-done | bytes 4194320 | tf_op jit(solution)/shard_map/all_gather | solution.py:72
  95.9 4.8 %convolution_convert_fusion.2 = bf16[256,4096]{1,0:T(8,128)(2,1)} fusion(bf16[256,512]{0,1:T(8,128)(2,1)S(1)} %bitcast.46, bf16[512,4096]{1,0:T(8,128)(2,1)} %all-gather.2.cloned.1.call-done), kind=kOutput, calls=%fused_computation.8 | convolution fusion | flops 1074790400 | bytes 6553600 | tf_op jit(solution)/shard_map/dot_general | solution.py:70
  100.7 0.1 reshape.132
  100.9 0.1 dynamic_slice.3
  100.9 0.2 fusion.2
  101.1 0.5 broadcast.80
  101.7 0.8 reduce.2
  102.5 0.8 reshape.134
  103.2 7.5 %all-to-all-start = ((bf16[32,2,2304]{2,1,0:T(2,128)(2,1)}), bf16[32,2,2304]{2,1,0:T(2,128)(2,1)S(1)}, u32[]{:S(2)}, u32[]{:S(2)}) async-start(bf16[32,2,2304]{2,1,0:T(2,128)(2,1)} %reshape.134), calls=%async_computation.1 | async-start | bytes 589824 | tf_op jit(solution)/shard_map/all_to_all | solution.py:90
  110.7 0.1 eq.44
  110.8 0.1 copy.40
  110.9 0.1 eq.45
  111.0 0.1 copy.41
  111.1 23.3 %all-to-all-done = bf16[32,2,2304]{2,1,0:T(2,128)(2,1)S(1)} async-done(((bf16[32,2,2304]{2,1,0:T(2,128)(2,1)}), bf16[32,2,2304]{2,1,0:T(2,128)(2,1)S(1)}, u32[]{:S(2)}, u32[]{:S(2)}) %all-to-all-start) | async-done | bytes 294944 | tf_op jit(solution)/shard_map/all_to_all | solution.py:90
  134.4 0.2 reshape.135
  134.7 0.2 convolution_convert_fusion.1
  134.8 0.7 reshape.133
  135.5 49.4 %reduce-scatter.2.cloned.1.call-done = bf16[16,4096]{1,0:T(8,128)(2,1)} async-done(((bf16[256,4096]{1,0:T(8,128)(2,1)}), bf16[16,4096]{1,0:T(8,128)(2,1)}) %reduce-scatter.2.cloned.1.call-update) | async-done | bytes 131088 | tf_op jit(solution)/shard_map/reduce_scatter | solution.py:75
  (19 shorter events, 0.2 us)
Async XLA Ops:
  7.2 25.2 %copy-start = (bf16[256,512]{1,0:T(8,128)(2,1)S(1)}, bf16[256,512]{1,0:T(8,128)(2,1)}, u32[]{:S(2)}) copy-start(bf16[256,512]{1,0:T(8,128)(2,1)} %param.9) | copy-start | bytes 786436
  7.2 88.7 %all-gather.2.cloned.1.call-start = ((), (), s32[]{:S(2)}) async-start(), calls=%async_computation.2 | async-start | bytes 4325376 | tf_op jit(solution)/shard_map/all_gather | solution.py:72
  7.9 177.1 %reduce-scatter.2.cloned.1.call-start = ((), (), s32[]{:S(2)}) async-start(), calls=%async_computation.3 | async-start | bytes 2228224 | tf_op jit(solution)/shard_map/reduce_scatter | solution.py:75
  8.6 25.8 %copy-start.1 = (bf16[2048,576]{0,1:T(8,128)(2,1)S(1)}, bf16[2048,576]{0,1:T(8,128)(2,1)}, u32[]{:S(2)}) copy-start(bf16[2048,576]{0,1:T(8,128)(2,1)} %param.11) | copy-start | bytes 7077892
  45.0 2.7 %copy-start.2 = (bf16[512,1024]{0,1:T(8,128)(2,1)S(1)}, bf16[512,1024]{0,1:T(8,128)(2,1)}, u32[]{:S(2)}) copy-start(bf16[512,1024]{0,1:T(8,128)(2,1)} %copy.34) | copy-start | bytes 3145732
  95.9 4.9 %copy-start.3 = (bf16[2,8,576]{2,1,0:T(8,128)(2,1)S(1)}, bf16[2,8,576]{2,1,0:T(8,128)(2,1)}, u32[]{:S(2)}) copy-start(bf16[2,8,576]{2,1,0:T(8,128)(2,1)} %param.12) | copy-start | bytes 55300
  95.9 5.0 %copy-start.5 = (s32[64]{0:T(128)S(1)}, s32[64]{0:T(128)}, u32[]{:S(2)}) copy-start(s32[64]{0:T(128)} %param.16) | copy-start | bytes 772
  95.9 15.1 %copy-start.4 = (s32[64]{0:T(128)S(1)}, s32[64]{0:T(128)}, u32[]{:S(2)}) copy-start(s32[64]{0:T(128)} %param.17) | copy-start | bytes 772
  103.2 31.2 %all-to-all-start = ((bf16[32,2,2304]{2,1,0:T(2,128)(2,1)}), bf16[32,2,2304]{2,1,0:T(2,128)(2,1)S(1)}, u32[]{:S(2)}, u32[]{:S(2)}) async-start(bf16[32,2,2304]{2,1,0:T(2,128)(2,1)} %reshape.134), calls=%async_computation.1 | async-start | bytes 589824 | tf_op jit(solution)/shard_map/all_to_all | solution.py:90
Sparse Core Ops, SparseCore 0:
  10.1 85.7 all-gather.1
  100.9 84.0 reduce-scatter.1
where the time goes:
time: 193 us; the launch traced here: 192 us
  waiting for transfers between devices  121 us (63%)
  blocking collectives  19.9 us (10%)
  between operations  14.9 us (8%)
  matrix products  14.2 us (7%)
  other arithmetic  7.54 us (4%)
  starting transfers between devices  7.53 us (4%)
  local copies, waits for them, and re-layouts  6.62 us (3%)
    reduce_scatter x1, waiting for transfers between devices, body(): lax.psum_scatter(partial_value.astype(jnp.bfloat16), 'tp', scatter_dimens...  49.4 us
    all_gather x1, waiting for transfers between devices, body(): lax.all_gather(out_proj, 'grp', axis=1, tiled=True)  47.7 us
    all_to_all x1, waiting for transfers between devices, body(): lax.all_to_all(outgoing, 'grp', split_axis=0, concat_axis=0, tiled=True)  23.3 us
    all_gather x1, blocking collectives, body(): lax.all_gather(new_latent, 'tp', axis=1, tiled=True).reshape(span, width)  19.9 us
    all_to_all x1, starting transfers between devices, body(): lax.all_to_all(outgoing, 'grp', split_axis=0, concat_axis=0, tiled=True)  7.45 us
    dot_general x1, matrix products, body(): jnp.dot(attended, lax.all_gather(out_proj, 'grp', axis=1, tiled=True), pr...  4.83 us
    unnamed x16, local copies, waits for them, and re-layouts  4.49 us
    dot_general x1, matrix products, attend_heads(): lax.dot_general(queries, key_rows, (((1,), (1,)), ((), ())), preferred_el...  4.47 us
  transfers between devices with their start and end apart: 3, of which 3 were waited for; matrix products, arithmetic and copies ran while one was open for 12% of the time, Pallas kernels for 0%

commit v1 on v0

v1 whole, which is shorter than its diff:
```python
import jax
import jax.numpy as jnp
from jax import lax
from jax.experimental import pallas as pl
from jax.experimental.pallas import tpu as pltpu
from jax.sharding import PartitionSpec as P

NOPE = 128
ROPE = 64
VDIM = 128
KVR = 512
KVW = 576
SLOTS = 4
SPAN = 256
PREFIX = 2048
KEYS = PREFIX + SPAN
HEADS_DEV = 4
GRP = 32
Z = 16
W_ROWS = 512
NL_ROWS = 80
BLK_ROWS = W_ROWS + NL_ROWS
CHUNKS = ((0, 304), (304, 288))
LAST = 15
MESH = pl.DeviceIdType.MESH
F32 = jnp.float32
BF16 = jnp.bfloat16


def kernel(
    len_ref, own_ref, slot_ref, qn_hbm, qr_hbm, cache_hbm, nl_hbm, up_hbm, w_hbm,
    mixed_ref, dec_ref,
    qn, qr, cache, up, nl, fresh, kv, ropes, ring, att, part, p1, mid, p2, res, res_in, dec, dec_in,
    in_sem, ring_send, ring_recv, nlx_send, nlx_recv, nly_send, nly_recv, att_sem,
    p1_send, p1_recv, p2_send, p2_recv, res_send, res_recv, dec_sem,
):
    g = lax.axis_index("grp")
    t = lax.axis_index("tp")
    z, core = g // 2, lax.rem(g, 2)
    x, y = t // 4, lax.rem(t, 4)
    up_z = {"grp": lax.rem(g + 2, GRP)}
    down_z = {"grp": lax.rem(g + GRP - 2, GRP)}
    sibling = {"grp": g + 1 - 2 * core}
    xs = [lax.rem(x + d, 4) for d in (1, 2, 3)]
    ys = [lax.rem(y + d, 4) for d in (1, 2, 3)]
    x_peers = [{"tp": xx * 4 + y} for xx in xs]
    y_peers = [{"tp": x * 4 + yy} for yy in ys]

    loads = [
        pltpu.make_async_copy(w_hbm, ring.at[0, pl.ds(0, W_ROWS)], in_sem.at[0]),
        pltpu.make_async_copy(nl_hbm, nl, in_sem.at[1]),
        pltpu.make_async_copy(up_hbm, up, in_sem.at[2]),
        pltpu.make_async_copy(cache_hbm, cache, in_sem.at[3]),
        pltpu.make_async_copy(qn_hbm, qn, in_sem.at[4]),
        pltpu.make_async_copy(qr_hbm, qr, in_sem.at[5]),
    ]
    for load in loads:
        load.start()
    barrier = pltpu.get_barrier_semaphore()
    partners = [up_z, down_z, sibling] + x_peers + y_peers
    for who in partners:
        pl.semaphore_signal(barrier, inc=1, device_id=who, device_id_type=MESH)
    loads[1].wait()
    rows = nl[...]
    tiles = [rows[:, k * 128 : (k + 1) * 128] for k in range(4)]
    tiles.append(jnp.concatenate([rows[:, KVR:], jnp.zeros((16, 64), BF16)], axis=1))
    packed = jnp.concatenate(tiles, axis=0)
    ring[0, pl.ds(W_ROWS, NL_ROWS), :] = packed
    fresh[x, y] = packed
    loads[0].wait()
    pl.semaphore_wait(barrier, len(partners))

    def remote(src, dst, send, recv, who):
        return pltpu.make_async_remote_copy(
            src_ref=src, dst_ref=dst, send_sem=send, recv_sem=recv, device_id=who, device_id_type=MESH
        )

    def hop(src, dst, k, who):
        at, n = CHUNKS[k]
        return remote(
            ring.at[src, pl.ds(at, n)], ring.at[dst, pl.ds(at, n)], ring_send.at[dst, k], ring_recv.at[dst, k], who
        )

    def send_first():
        for k in range(len(CHUNKS)):
            hop(0, 1, k, up_z).start()
            hop(0, 8, k, down_z).start()

    def service(s):
        for k in range(len(CHUNKS)):
            hop(s - 1, s, k, up_z).wait_recv()
            if s < 7:
                hop(s, s + 1, k, up_z).start()
            elif k < len(CHUNKS) // 2:
                hop(s, LAST, k, up_z).start()
            hop(s + 6, s + 7, k, down_z).wait_recv()
            if s < 7:
                hop(s + 7, s + 8, k, down_z).start()
            elif k >= len(CHUNKS) // 2:
                hop(s + 7, LAST, k, down_z).start()

    def service_last():
        for k in range(len(CHUNKS)):
            hop(7, LAST, k, up_z).wait_recv()

    def nlx(i):
        return remote(fresh.at[x, y], fresh.at[x, y], nlx_send.at[i], nlx_recv.at[i], x_peers[i])

    def nlx_from(i):
        src = lax.rem(x + 3 - i, 4)
        return remote(fresh.at[src, y], fresh.at[src, y], nlx_send.at[i], nlx_recv.at[i], x_peers[i])

    def nly(i):
        return remote(fresh.at[:, y], fresh.at[:, y], nly_send.at[i], nly_recv.at[i], y_peers[i])

    def nly_from(i):
        src = lax.rem(y + 3 - i, 4)
        return remote(fresh.at[:, src], fresh.at[:, src], nly_send.at[i], nly_recv.at[i], y_peers[i])

    for i in range(3):
        nlx(i).start()
    send_first()

    def project_keys(lat, rope, at, n):
        kv[pl.ds(at, n), :] = jnp.dot(lat, up[...], preferred_element_type=F32).astype(BF16)
        zero = jnp.zeros((n, 64), BF16)
        ropes[0, pl.ds(at, n), :] = jnp.concatenate([rope, zero], axis=1)
        ropes[1, pl.ds(at, n), :] = jnp.concatenate([zero, rope], axis=1)

    for i in (2, 3):
        loads[i].wait()

    def prefix_keys(i, _):
        at = pl.multiple_of(i * 256, 256)
        project_keys(cache[pl.ds(at, 256), :KVR], cache[pl.ds(at, 256), KVR:], at, 256)
        return _

    lax.fori_loop(0, 4, prefix_keys, 0)
    for i in range(3):
        nlx_from(i).wait_recv()
    for i in range(3):
        nly(i).start()
    lax.fori_loop(4, 8, prefix_keys, 0)
    service(1)
    for i in range(3):
        nly_from(i).wait_recv()
    new = fresh[...].reshape(16, 5, 16, 128)
    new = [new[:, k].reshape(SPAN, 128) for k in range(5)]
    project_keys(jnp.concatenate(new[:4], axis=1), new[4][:, :64], PREFIX, SPAN)

    for i in (4, 5):
        loads[i].wait()
    to_bits = (NOPE + ROPE) ** -0.5 * 1.4426950408889634
    col = lax.broadcasted_iota(jnp.int32, (1, PREFIX), 1)
    old_bias = jnp.where(col < len_ref[0], 0.0, -1e30).astype(F32)
    row = lax.broadcasted_iota(jnp.int32, (SPAN, SPAN), 0)
    key = lax.broadcasted_iota(jnp.int32, (SPAN, SPAN), 1)
    token = ((key // 8) % 2) * 128 + (key // 16) * 8 + key % 8
    new_bias = jnp.where(token <= row, 0.0, -1e30).astype(F32)

    def head(h):
        k = jnp.concatenate([kv[:, h * 256 : h * 256 + NOPE], ropes[h % 2]], axis=1)
        pair = h // 2
        q = jnp.concatenate([qn[:, h * 128 : (h + 1) * 128], qr[:, pair * 128 : (pair + 1) * 128]], axis=1)
        s = lax.dot_general(q, k, (((1,), (1,)), ((), ())), preferred_element_type=F32)
        s = jnp.concatenate([s[:, :PREFIX] + old_bias, s[:, PREFIX:] + new_bias], axis=1)
        highest = jnp.max(s, axis=1, keepdims=True)
        e = jnp.exp2((s - highest) * to_bits)
        total = jnp.sum(e, axis=1, keepdims=True)
        v = kv[:, h * 256 + NOPE : (h + 1) * 256]
        o = jnp.dot(e.astype(BF16), v, preferred_element_type=F32)
        att[0, :, h * 128 : (h + 1) * 128] = (o / total).astype(BF16)

    head(0)
    service(2)
    head(1)
    head(2)
    service(3)
    head(3)
    swap = remote(att.at[0], att.at[1], att_sem.at[0], att_sem.at[1], sibling)
    swap.start()
    swap.wait_recv()

    def plane_of(b):
        if b < 8:
            return lax.rem(z + Z - b, Z)
        if b == LAST:
            return lax.rem(z + 8, Z)
        return lax.rem(z + b - 7, Z)

    def out_first(b, i):
        src = part.at[b, :, xs[i]] if b < 8 else part.at[b, :, :, ys[i]]
        who = x_peers[i] if b < 8 else y_peers[i]
        return remote(src, p1.at[b, i], p1_send.at[b, i], p1_recv.at[b, i], who)

    def out_second(b, i):
        src = mid.at[b, :, ys[i]] if b < 8 else mid.at[b, :, xs[i]]
        who = y_peers[i] if b < 8 else x_peers[i]
        return remote(src, p2.at[b, i], p2_send.at[b, i], p2_recv.at[b, i], who)

    def out_res(b):
        return remote(res.at[b], res_in.at[b], res_send.at[b], res_recv.at[b], sibling)

    def project(blocks):
        w = jnp.concatenate([ring[b, pl.ds(0, W_ROWS), :] for b in blocks], axis=1)
        a = att[...].reshape(2 * SPAN, W_ROWS)
        o = jnp.dot(a, w, preferred_element_type=F32).astype(BF16)
        for n, b in enumerate(blocks):
            part[b] = o[:, n * 128 : (n + 1) * 128].reshape(2, 4, 4, 16, 128)
        for i in range(3):
            for b in blocks:
                out_first(b, i).start()

    def first_sum(blocks):
        for b in blocks:
            for i in range(3):
                out_first(b, i).wait_recv()
            own = part[b, :, x] if b < 8 else part[b, :, :, y]
            total = own.astype(F32)
            for i in range(3):
                total += p1[b, i].astype(F32)
            mid[b] = total.astype(BF16)
            for i in range(3):
                out_second(b, i).start()

    def second_sum(blocks):
        for b in blocks:
            for i in range(3):
                out_second(b, i).wait_recv()
            own = mid[b, :, y] if b < 8 else mid[b, :, x]
            total = own.astype(F32)
            for i in range(3):
                total += p2[b, i].astype(F32)
            total = total.astype(BF16)
            res[b] = total[1]
            out_res(b).start()
            at = pl.multiple_of((2 * plane_of(b) + core) * 128, 128)
            mixed_ref[:, pl.ds(at, 128)] = total[0]

    def collect(blocks):
        for b in blocks:
            out_res(b).wait_recv()
            at = pl.multiple_of((2 * plane_of(b) + 1 - core) * 128, 128)
            mixed_ref[:, pl.ds(at, 128)] = res_in[b]

    steps = [(0,)] + [(s, s + 7) for s in range(1, 8)] + [(LAST,)]
    done = 3
    for s in range(9):
        if s > done:
            if s < 8:
                service(s)
            else:
                service_last()
        project(steps[s])
        if s >= 1:
            first_sum(steps[s - 1])
        if s >= 2:
            second_sum(steps[s - 2])
    first_sum(steps[8])
    second_sum(steps[7])

    def pick(owner, s):
        def look(b, carry):
            slot, half = carry
            plane, i = b // 2, lax.rem(b, 2)
            block = 2 * (2 * plane + core) + i
            hit = jnp.logical_and(own_ref[block] == owner, slot_ref[block] == s)
            away = lax.rem(z - plane + Z, Z)
            place = jnp.where(away < 8, away, jnp.where(away == 8, LAST, 23 - away))
            return jnp.where(hit, place, slot), jnp.where(hit, i, half)

        slot, half = lax.fori_loop(0, 2 * Z, look, (jnp.int32(-1), jnp.int32(0)))
        got = ring[jnp.maximum(slot, 0), pl.ds(W_ROWS, NL_ROWS), :].reshape(5, 16, 128).astype(F32)
        got = jnp.where(half == 0, got[:, :8], got[:, 8:])
        got = jnp.where(slot >= 0, got, 0.0)
        return jnp.concatenate([got[k] for k in range(5)], axis=1)

    for s in range(0, SLOTS, 2):
        both = jnp.concatenate([pick(g + 1 - 2 * core, s), pick(g + 1 - 2 * core, s + 1)], axis=0)
        dec[s // 2] = both.astype(BF16)
    swap_dec = remote(dec, dec_in, dec_sem.at[0], dec_sem.at[1], sibling)
    swap_dec.start()
    mine = [pick(g, s) for s in range(SLOTS)]
    swap_dec.wait_recv()
    for s in range(SLOTS):
        other = dec_in[s // 2].astype(F32)[(s % 2) * 8 : (s % 2) * 8 + 8]
        dec_ref[s] = (mine[s] + other)[:, :KVW].astype(BF16)

    second_sum(steps[8])
    for blocks in steps:
        collect(blocks)

    for k in range(len(CHUNKS)):
        for s in range(7):
            hop(s, s + 1, k, up_z).wait_send()
            hop(s + 7 if s else 0, s + 8, k, down_z).wait_send()
        hop(7, LAST, k, up_z).wait_send()
    for i in range(3):
        nlx(i).wait_send()
        nly(i).wait_send()
    swap.wait_send()
    swap_dec.wait_send()
    for b in range(16):
        for i in range(3):
            out_first(b, i).wait_send()
            out_second(b, i).wait_send()
        out_res(b).wait_send()


def body(query_nope, query_rope, latent_cache, new_latent, prefix_length, latent_up, out_proj, owners, slot_index):
    nl = new_latent.reshape(16, KVW)
    smem = pl.BlockSpec(memory_space=pltpu.SMEM)
    hbm = pl.BlockSpec(memory_space=pl.ANY)
    vmem = pl.BlockSpec(memory_space=pltpu.VMEM)
    dma = pltpu.SemaphoreType.DMA
    nk = len(CHUNKS)
    return pl.pallas_call(
        kernel,
        out_shape=(
            jax.ShapeDtypeStruct((16, 4096), BF16),
            jax.ShapeDtypeStruct((SLOTS, 8, KVW), BF16),
        ),
        in_specs=[smem] * 3 + [hbm] * 6,
        out_specs=(vmem, vmem),
        scratch_shapes=[
            pltpu.VMEM((SPAN, 512), BF16),
            pltpu.VMEM((SPAN, 256), BF16),
            pltpu.VMEM((PREFIX, KVW), BF16),
            pltpu.VMEM((KVR, 1024), BF16),
            pltpu.VMEM((16, KVW), BF16),
            pltpu.VMEM((4, 4, NL_ROWS, 128), BF16),
            pltpu.VMEM((KEYS, 1024), BF16),
            pltpu.VMEM((2, KEYS, 128), BF16),
            pltpu.VMEM((16, BLK_ROWS, 128), BF16),
            pltpu.VMEM((2, SPAN, 512), BF16),
            pltpu.VMEM((16, 2, 4, 4, 16, 128), BF16),
            pltpu.VMEM((16, 3, 2, 4, 16, 128), BF16),
            pltpu.VMEM((16, 2, 4, 16, 128), BF16),
            pltpu.VMEM((16, 3, 2, 16, 128), BF16),
            pltpu.VMEM((16, 16, 128), BF16),
            pltpu.VMEM((16, 16, 128), BF16),
            pltpu.VMEM((2, 16, 640), BF16),
            pltpu.VMEM((2, 16, 640), BF16),
            dma((6,)),
            dma((16, nk)),
            dma((16, nk)),
            dma((3,)),
            dma((3,)),
            dma((3,)),
            dma((3,)),
            dma((2,)),
            dma((16, 3)),
            dma((16, 3)),
            dma((16, 3)),
            dma((16, 3)),
            dma((16,)),
            dma((16,)),
            dma((2,)),
        ],
        compiler_params=pltpu.CompilerParams(
            collective_id=0, has_side_effects=True, vmem_limit_bytes=56 * 1024 * 1024
        ),
        cost_estimate=pl.CostEstimate(flops=5_000_000_000, bytes_accessed=6_000_000, transcendentals=2_400_000),
    )(prefix_length, owners, slot_index, query_nope, query_rope, latent_cache, nl, latent_up, out_proj)


def solution(mesh):
    placed = (
        P("grp", "tp"),
        P("grp", "tp"),
        P("grp", None),
        P("grp", "tp", None),
        P("grp"),
        P(None, "tp"),
        P("tp", "grp"),
        P(),
        P(),
    )
    return jax.shard_map(
        body,
        mesh=mesh,
        in_specs=placed,
        out_specs=(P(("grp", "tp"), None), P("grp", "tp", None)),
        check_vma=False,
    )
```

time: 193 us -> 83.7 us (0.43)
  waiting for transfers between devices: 121 us -> 0 us
  Pallas kernels: 0 us -> 74.8 us
  blocking collectives: 19.9 us -> 0 us
  matrix products: 14.2 us -> 0 us
  between operations: 14.9 us -> 1.29 us
  other arithmetic: 7.54 us -> 0 us
  starting transfers between devices: 7.53 us -> 0 us
    pallas_call x0 -> x1, Pallas kernels: none -> 74.8 us  [body(): pl.pallas_call(kernel, out_shape=(jax.ShapeDtypeStruct((16, 4096), BF16),...]
    reduce_scatter x1 -> x0, waiting for transfers between devices: 49.4 us -> none  [body(): lax.psum_scatter(partial_value.astype(jnp.bfloat16), 'tp', scatter_dimens...]
    all_gather x1 -> x0, waiting for transfers between devices: 47.7 us -> none  [body(): lax.all_gather(out_proj, 'grp', axis=1, tiled=True)]
    all_to_all x1 -> x0, waiting for transfers between devices: 23.3 us -> none  [body(): lax.all_to_all(outgoing, 'grp', split_axis=0, concat_axis=0, tiled=True)]
    all_gather x1 -> x0, blocking collectives: 19.9 us -> none  [body(): lax.all_gather(new_latent, 'tp', axis=1, tiled=True).reshape(span, width)]
    dot_general x7 -> x0, matrix products: 14.2 us -> none  [the longest x1 4.83 us: body(): jnp.dot(attended, lax.all_gather(out_proj, 'grp', axis=1, tiled=True), pr...]
    all_to_all x1 -> x0, starting transfers between devices: 7.45 us -> none  [body(): lax.all_to_all(outgoing, 'grp', split_axis=0, concat_axis=0, tiled=True)]
    convert_element_type x1 -> x0, other arithmetic: 3.42 us -> none  [attend_heads(): (expo / jnp.sum(expo, axis=2, keepdims=True)).astype(jnp.bfloat16)]
  transfers between devices with their start and end apart: 3 -> 0, of which waited for: 3 -> 0; matrix products, arithmetic and copies ran while one was open for 12% -> 0% of each run, Pallas kernels for 0% -> 0%
where the time goes in v1:
time: 83.7 us; the launch traced here: 83.4 us
  Pallas kernels  74.8 us (89%)
  local copies, waits for them, and re-layouts  7.31 us (9%)
  between operations  1.29 us (2%)
    pallas_call x1, Pallas kernels, body(): pl.pallas_call(kernel, out_shape=(jax.ShapeDtypeStruct((16, 4096), BF16),...  74.8 us
    unnamed x3, local copies, waits for them, and re-layouts  7.31 us

profile of v1, /device:TPU:1, one launch (start us, length us, event | category | flops | bytes accessed | tf_op | source)
XLA Modules:
  0.0 83.4 jit_solution(9461005397151940394)
XLA Ops:
  1.3 4.3 %copy.11.cache_hbm = bf16[2048,576]{1,0:T(8,128)(2,1)} copy(bf16[2048,576]{0,1:T(8,128)(2,1)} %param.11) | data formatting | bytes 4718592 | tf_op args[2]
  5.6 74.8 %shard_map.104 = (bf16[16,4096]{1,0:T(8,128)(2,1)}, bf16[4,8,576]{2,1,0:T(8,128)(2,1)}) custom-call(s32[1]{0:T(128)S(6)} %copy.14.len_ref, s32[64]{0:T(128)} %own_ref.1, s32[64]{0:T(128)} %slot_ref.1, bf16[256,512]{1,0:T(8,128)(2,1)} %qn_hbm.1, bf16[256,256]{1,0:T(8,128)(2,1)} %qr_hbm.1, bf16[2048,576]{1,0:T(8,128)(2,1)} %copy.11.cache_hbm, ...), custom_call_target="tpu_custom_call" | custom-call | flops 5000000000 | bytes 6000000 | tf_op jit(solution)/shard_map/pallas_call | solution.py:317
  80.4 1.6 %copy.15 = bf16[16,4096]{1,0:T(8,128)(2,1)} copy(bf16[16,4096]{1,0:T(8,128)(2,1)} %get-tuple-element.4) | data formatting | bytes 262144
  82.0 1.4 %copy.16 = bf16[4,8,576]{2,1,0:T(8,128)(2,1)} copy(bf16[4,8,576]{2,1,0:T(8,128)(2,1)} %get-tuple-element.5) | data formatting | bytes 73728

commit v2 on v1

v2 whole, which is shorter than its diff:
```python
import jax
import jax.numpy as jnp
from jax import lax
from jax.experimental import pallas as pl
from jax.experimental.pallas import tpu as pltpu
from jax.sharding import PartitionSpec as P

NOPE = 128
ROPE = 64
VDIM = 128
KVR = 512
KVW = 576
SLOTS = 4
SPAN = 256
PREFIX = 2048
KEYS = PREFIX + SPAN
HEADS_DEV = 4
GRP = 32
Z = 16
W_ROWS = 512
NL_ROWS = 80
BLK_ROWS = W_ROWS + NL_ROWS
CHUNKS = ((0, 304), (304, 288))
DIRECT = (7, 14, 15)
LAST = 15
MESH = pl.DeviceIdType.MESH
F32 = jnp.float32
BF16 = jnp.bfloat16


def kernel(
    len_ref, own_ref, slot_ref, qn_hbm, qr_hbm, cache_hbm, nl_hbm, up_hbm, w_hbm,
    mixed_ref, dec_ref,
    qn, qr, cache, up, nl, fresh, up_t, kv, ropes, ring, att, part, p1, mid, p2, direct, res, res_in, dec, dec_in,
    in_sem, ring_send, ring_recv, nl_sem, att_sem,
    p1_send, p1_recv, p2_send, p2_recv, direct_send, direct_recv, res_send, res_recv, dec_sem,
):
    g = lax.axis_index("grp")
    t = lax.axis_index("tp")
    z, core = g // 2, lax.rem(g, 2)
    x, y = t // 4, lax.rem(t, 4)
    up_z = {"grp": lax.rem(g + 2, GRP)}
    down_z = {"grp": lax.rem(g + GRP - 2, GRP)}
    sibling = {"grp": g + 1 - 2 * core}
    xs = [lax.rem(x + d, 4) for d in (1, 2, 3)]
    ys = [lax.rem(y + d, 4) for d in (1, 2, 3)]
    x_peers = [{"tp": xx * 4 + y} for xx in xs]
    y_peers = [{"tp": x * 4 + yy} for yy in ys]

    loads = [
        pltpu.make_async_copy(w_hbm, ring.at[0, pl.ds(0, W_ROWS)], in_sem.at[0]),
        pltpu.make_async_copy(nl_hbm, nl, in_sem.at[1]),
        pltpu.make_async_copy(up_hbm, up, in_sem.at[2]),
        pltpu.make_async_copy(cache_hbm, cache, in_sem.at[3]),
        pltpu.make_async_copy(qn_hbm, qn, in_sem.at[4]),
        pltpu.make_async_copy(qr_hbm, qr, in_sem.at[5]),
    ]
    for load in loads:
        load.start()
    barrier = pltpu.get_barrier_semaphore()
    plane = [(dx, dy) for dx in range(4) for dy in range(4)][1:]
    plane_xy = [(lax.rem(x + dx, 4), lax.rem(y + dy, 4)) for dx, dy in plane]
    plane_peers = [{"tp": xx * 4 + yy} for xx, yy in plane_xy]
    partners = [up_z, down_z, sibling] + plane_peers
    for who in partners:
        pl.semaphore_signal(barrier, inc=1, device_id=who, device_id_type=MESH)
    loads[1].wait()
    rows = nl[...]
    tiles = [rows[:, k * 128 : (k + 1) * 128] for k in range(4)]
    tiles.append(jnp.concatenate([rows[:, KVR:], jnp.zeros((16, 64), BF16)], axis=1))
    packed = jnp.concatenate(tiles, axis=0)
    ring[0, pl.ds(W_ROWS, NL_ROWS), :] = packed
    fresh[t] = packed
    loads[0].wait()
    pl.semaphore_wait(barrier, len(partners))

    def remote(src, dst, send, recv, who):
        return pltpu.make_async_remote_copy(
            src_ref=src, dst_ref=dst, send_sem=send, recv_sem=recv, device_id=who, device_id_type=MESH
        )

    def hop(src, dst, k, who):
        at, n = CHUNKS[k]
        return remote(
            ring.at[src, pl.ds(at, n)], ring.at[dst, pl.ds(at, n)], ring_send.at[dst, k], ring_recv.at[dst, k], who
        )

    def send_first():
        for k in range(len(CHUNKS)):
            hop(0, 1, k, up_z).start()
            hop(0, 8, k, down_z).start()

    def service(s, k):
        hop(s - 1, s, k, up_z).wait_recv()
        if s < 7:
            hop(s, s + 1, k, up_z).start()
        elif k == 0:
            hop(s, LAST, k, up_z).start()
        hop(s + 6, s + 7, k, down_z).wait_recv()
        if s < 7:
            hop(s + 7, s + 8, k, down_z).start()
        elif k == 1:
            hop(s + 7, LAST, k, down_z).start()

    def service_last():
        for k in range(len(CHUNKS)):
            hop(7, LAST, k, up_z).wait_recv()

    def new_rows(i):
        return remote(fresh.at[t], fresh.at[t], nl_sem.at[0], nl_sem.at[1], plane_peers[i])

    others = fresh.at[pl.ds(0, 15)]
    all_new_rows = remote(others, others, nl_sem.at[0], nl_sem.at[1], plane_peers[0])

    send_first()
    for i in range(15):
        new_rows(i).start()

    def look(b, codes):
        plane, i = b // 2, lax.rem(b, 2)
        block = 2 * (2 * plane + core) + i
        owner, place = own_ref[block], slot_ref[block]
        away = lax.rem(z - plane + Z, Z)
        code = 2 * jnp.where(away < 8, away, jnp.where(away == 8, LAST, 23 - away)) + i
        wanted = [(who, s) for who in (g, g + 1 - 2 * core) for s in range(SLOTS)]
        return tuple(
            jnp.where(jnp.logical_and(owner == who, place == s), code, old)
            for (who, s), old in zip(wanted, codes, strict=True)
        )

    codes = lax.fori_loop(0, 2 * Z, look, (jnp.int32(-1),) * (2 * SLOTS))

    def rope_rows(rope, at, n):
        zero = jnp.zeros((64, n), BF16)
        ropes[0, :, pl.ds(at, n)] = jnp.concatenate([rope, zero], axis=0)
        ropes[1, :, pl.ds(at, n)] = jnp.concatenate([zero, rope], axis=0)

    for i in (2, 3):
        loads[i].wait()

    up_t[...] = up[...].T

    def prefix_keys(i, _):
        at = pl.multiple_of(i * 256, 256)
        kv[:, pl.ds(at, 256)] = jnp.dot(
            up_t[...], cache[pl.ds(0, KVR), pl.ds(at, 256)], preferred_element_type=F32
        ).astype(BF16)
        rope_rows(cache[pl.ds(KVR, ROPE), pl.ds(at, 256)], at, 256)
        return _

    lax.fori_loop(0, 8, prefix_keys, 0)
    service(1, 0)
    all_new_rows.wait_recv()
    new = fresh[...].reshape(16, 5, 16, 128)
    new = [new[:, k].reshape(SPAN, 128) for k in range(5)]
    kv[:, pl.ds(PREFIX, SPAN)] = lax.dot_general(
        up_t[...], jnp.concatenate(new[:4], axis=1), (((1,), (1,)), ((), ())), preferred_element_type=F32
    ).astype(BF16)
    rope_rows(new[4].T[:ROPE], PREFIX, SPAN)

    service(1, 1)
    for i in (4, 5):
        loads[i].wait()
    to_bits = (NOPE + ROPE) ** -0.5 * 1.4426950408889634
    col = lax.broadcasted_iota(jnp.int32, (1, PREFIX), 1)
    old_bias = jnp.where(col < len_ref[0], 0.0, -1e30).astype(F32)
    row = lax.broadcasted_iota(jnp.int32, (SPAN, SPAN), 0)
    key = lax.broadcasted_iota(jnp.int32, (SPAN, SPAN), 1)
    token = ((key // 8) % 2) * 128 + (key // 16) * 8 + key % 8
    new_bias = jnp.where(token <= row, 0.0, -1e30).astype(F32)

    def head(h):
        k = jnp.concatenate([kv[h * 256 : h * 256 + NOPE], ropes[h % 2]], axis=0)
        pair = h // 2
        q = jnp.concatenate([qn[:, h * 128 : (h + 1) * 128], qr[:, pair * 128 : (pair + 1) * 128]], axis=1)
        s = jnp.dot(q, k, preferred_element_type=F32)
        s = jnp.concatenate([s[:, :PREFIX] + old_bias, s[:, PREFIX:] + new_bias], axis=1)
        highest = jnp.max(s, axis=1, keepdims=True)
        e = jnp.exp2((s - highest) * to_bits)
        total = jnp.sum(e, axis=1, keepdims=True)
        v = kv[h * 256 + NOPE : (h + 1) * 256]
        o = lax.dot_general(e.astype(BF16), v, (((1,), (1,)), ((), ())), preferred_element_type=F32)
        att[0, :, h * 128 : (h + 1) * 128] = (o / total).astype(BF16)

    head(0)
    service(2, 0)
    head(1)
    service(2, 1)
    head(2)
    service(3, 0)
    head(3)
    swap = remote(att.at[0], att.at[1], att_sem.at[0], att_sem.at[1], sibling)
    swap.start()

    def plane_of(b):
        if b < 8:
            return lax.rem(z + Z - b, Z)
        if b == LAST:
            return lax.rem(z + 8, Z)
        return lax.rem(z + b - 7, Z)

    def out_first(b, i):
        src = part.at[b, :, xs[i]] if b < 8 else part.at[b, :, :, ys[i]]
        who = x_peers[i] if b < 8 else y_peers[i]
        return remote(src, p1.at[b, i], p1_send.at[b, i], p1_recv.at[b, i], who)

    def out_second(b, i):
        src = mid.at[b, :, ys[i]] if b < 8 else mid.at[b, :, xs[i]]
        who = y_peers[i] if b < 8 else x_peers[i]
        return remote(src, p2.at[b, i], p2_send.at[b, i], p2_recv.at[b, i], who)

    def out_direct(b, i):
        n = DIRECT.index(b)
        xx, yy = plane_xy[i]
        return remote(
            part.at[b, :, xx, yy], direct.at[n, i], direct_send.at[n], direct_recv.at[n], plane_peers[i]
        )

    def all_direct(b):
        n = DIRECT.index(b)
        return remote(direct.at[n], direct.at[n], direct_send.at[n], direct_recv.at[n], plane_peers[0])

    def out_res(b):
        return remote(res.at[b], res_in.at[b], res_send.at[b], res_recv.at[b], sibling)

    def project(blocks):
        w = jnp.concatenate([ring[b, pl.ds(0, W_ROWS), :] for b in blocks], axis=1)
        a = att[...].reshape(2 * SPAN, W_ROWS)
        o = jnp.dot(a, w, preferred_element_type=F32).astype(BF16)
        for n, b in enumerate(blocks):
            part[b] = o[:, n * 128 : (n + 1) * 128].reshape(2, 4, 4, 16, 128)
        for i in range(15 if blocks[0] in DIRECT else 3):
            for b in blocks:
                if b in DIRECT:
                    out_direct(b, i).start()
                else:
                    out_first(b, i).start()

    def first_sum(blocks):
        for b in blocks:
            for i in range(3):
                out_first(b, i).wait_recv()
            own = part[b, :, x] if b < 8 else part[b, :, :, y]
            total = own.astype(F32)
            for i in range(3):
                total += p1[b, i].astype(F32)
            mid[b] = total.astype(BF16)
            for i in range(3):
                out_second(b, i).start()

    def deliver(b, total):
        res[b] = total[1]
        out_res(b).start()
        at = pl.multiple_of((2 * plane_of(b) + core) * 128, 128)
        mixed_ref[:, pl.ds(at, 128)] = total[0]

    def direct_sum(blocks):
        for b in blocks:
            all_direct(b).wait_recv()
            total = part[b, :, x, y].astype(F32)
            for i in range(15):
                total += direct[DIRECT.index(b), i].astype(F32)
            deliver(b, total.astype(BF16))

    def second_sum(blocks):
        for b in blocks:
            for i in range(3):
                out_second(b, i).wait_recv()
            own = mid[b, :, y] if b < 8 else mid[b, :, x]
            total = own.astype(F32)
            for i in range(3):
                total += p2[b, i].astype(F32)
            deliver(b, total.astype(BF16))

    def collect(blocks):
        for b in blocks:
            out_res(b).wait_recv()
            at = pl.multiple_of((2 * plane_of(b) + 1 - core) * 128, 128)
            mixed_ref[:, pl.ds(at, 128)] = res_in[b]

    steps = [(0,)] + [(s, s + 7) for s in range(1, 8)] + [(LAST,)]
    service(3, 1)
    swap.wait_recv()
    project(steps[0])
    project(steps[1])
    service(4, 0)
    project(steps[2])
    project(steps[3])
    service(4, 1)
    project(steps[4])
    first_sum(steps[0] + steps[1])
    service(5, 0)
    first_sum(steps[2] + steps[3])
    service(5, 1)
    project(steps[5])
    second_sum(steps[0] + steps[1])
    service(6, 0)
    first_sum(steps[4])
    second_sum(steps[2] + steps[3])
    service(6, 1)
    project(steps[6])
    service(7, 0)
    first_sum(steps[5])
    second_sum(steps[4])
    service(7, 1)
    project(steps[7])
    first_sum(steps[6])
    second_sum(steps[5])
    service_last()
    project(steps[8])
    second_sum(steps[6])
    direct_sum(steps[7])

    def pick(code):
        got = ring[jnp.maximum(code, 0) // 2, pl.ds(W_ROWS, NL_ROWS), :].reshape(5, 16, 128).astype(F32)
        got = jnp.where(lax.rem(jnp.maximum(code, 0), 2) == 0, got[:, :8], got[:, 8:])
        got = jnp.where(code >= 0, got, 0.0)
        return jnp.concatenate([got[k] for k in range(5)], axis=1)

    for s in range(0, SLOTS, 2):
        both = jnp.concatenate([pick(codes[SLOTS + s]), pick(codes[SLOTS + s + 1])], axis=0)
        dec[s // 2] = both.astype(BF16)
    swap_dec = remote(dec, dec_in, dec_sem.at[0], dec_sem.at[1], sibling)
    swap_dec.start()
    mine = [pick(codes[s]) for s in range(SLOTS)]
    swap_dec.wait_recv()
    for s in range(SLOTS):
        other = dec_in[s // 2].astype(F32)[(s % 2) * 8 : (s % 2) * 8 + 8]
        dec_ref[s] = (mine[s] + other)[:, :KVW].astype(BF16)

    direct_sum(steps[8])
    for blocks in steps:
        collect(blocks)

    for k in range(len(CHUNKS)):
        for s in range(7):
            hop(s, s + 1, k, up_z).wait_send()
            hop(s + 7 if s else 0, s + 8, k, down_z).wait_send()
        hop(7, LAST, k, up_z).wait_send()
    all_new_rows.wait_send()
    swap.wait_send()
    swap_dec.wait_send()
    for b in range(16):
        if b in DIRECT:
            all_direct(b).wait_send()
        else:
            for i in range(3):
                out_first(b, i).wait_send()
                out_second(b, i).wait_send()
        out_res(b).wait_send()


def body(query_nope, query_rope, latent_cache, new_latent, prefix_length, latent_up, out_proj, owners, slot_index):
    nl = new_latent.reshape(16, KVW)
    cache = latent_cache.T
    smem = pl.BlockSpec(memory_space=pltpu.SMEM)
    hbm = pl.BlockSpec(memory_space=pl.ANY)
    vmem = pl.BlockSpec(memory_space=pltpu.VMEM)
    dma = pltpu.SemaphoreType.DMA
    nk = len(CHUNKS)
    return pl.pallas_call(
        kernel,
        out_shape=(
            jax.ShapeDtypeStruct((16, 4096), BF16),
            jax.ShapeDtypeStruct((SLOTS, 8, KVW), BF16),
        ),
        in_specs=[smem] * 3 + [hbm] * 6,
        out_specs=(vmem, vmem),
        scratch_shapes=[
            pltpu.VMEM((SPAN, 512), BF16),
            pltpu.VMEM((SPAN, 256), BF16),
            pltpu.VMEM((KVW, PREFIX), BF16),
            pltpu.VMEM((KVR, 1024), BF16),
            pltpu.VMEM((16, KVW), BF16),
            pltpu.VMEM((16, NL_ROWS, 128), BF16),
            pltpu.VMEM((1024, KVR), BF16),
            pltpu.VMEM((1024, KEYS), BF16),
            pltpu.VMEM((2, 128, KEYS), BF16),
            pltpu.VMEM((16, BLK_ROWS, 128), BF16),
            pltpu.VMEM((2, SPAN, 512), BF16),
            pltpu.VMEM((16, 2, 4, 4, 16, 128), BF16),
            pltpu.VMEM((16, 3, 2, 4, 16, 128), BF16),
            pltpu.VMEM((16, 2, 4, 16, 128), BF16),
            pltpu.VMEM((16, 3, 2, 16, 128), BF16),
            pltpu.VMEM((len(DIRECT), 15, 2, 16, 128), BF16),
            pltpu.VMEM((16, 16, 128), BF16),
            pltpu.VMEM((16, 16, 128), BF16),
            pltpu.VMEM((2, 16, 640), BF16),
            pltpu.VMEM((2, 16, 640), BF16),
            dma((6,)),
            dma((16, nk)),
            dma((16, nk)),
            dma((2,)),
            dma((2,)),
            dma((16, 3)),
            dma((16, 3)),
            dma((16, 3)),
            dma((16, 3)),
            dma((len(DIRECT),)),
            dma((len(DIRECT),)),
            dma((16,)),
            dma((16,)),
            dma((2,)),
        ],
        compiler_params=pltpu.CompilerParams(
            collective_id=0, has_side_effects=True, vmem_limit_bytes=56 * 1024 * 1024
        ),
        cost_estimate=pl.CostEstimate(flops=5_000_000_000, bytes_accessed=6_000_000, transcendentals=2_400_000),
    )(prefix_length, owners, slot_index, query_nope, query_rope, cache, nl, latent_up, out_proj)


def solution(mesh):
    placed = (
        P("grp", "tp"),
        P("grp", "tp"),
        P("grp", None),
        P("grp", "tp", None),
        P("grp"),
        P(None, "tp"),
        P("tp", "grp"),
        P(),
        P(),
    )
    return jax.shard_map(
        body,
        mesh=mesh,
        in_specs=placed,
        out_specs=(P(("grp", "tp"), None), P("grp", "tp", None)),
        check_vma=False,
    )
```

time: 83.7 us -> 67.7 us (0.81)
  Pallas kernels: 74.8 us -> 63.2 us
  local copies, waits for them, and re-layouts: 7.31 us -> 2.97 us
    pallas_call x1, Pallas kernels: 74.8 us -> 63.2 us  [body(): pl.pallas_call(kernel, out_shape=(jax.ShapeDtypeStruct((16, 4096), BF16),...]
    unnamed x3 -> x2, local copies, waits for them, and re-layouts: 7.31 us -> 2.97 us
where the time goes in v2:
time: 67.7 us; the launch traced here: 67.4 us
  Pallas kernels  63.2 us (93%)
  local copies, waits for them, and re-layouts  2.97 us (4%)
  between operations  1.29 us (2%)
    pallas_call x1, Pallas kernels, body(): pl.pallas_call(kernel, out_shape=(jax.ShapeDtypeStruct((16, 4096), BF16),...  63.2 us
    unnamed x2, local copies, waits for them, and re-layouts  2.97 us

profile of v2, /device:TPU:1, one launch (start us, length us, event | category | flops | bytes accessed | tf_op | source)
XLA Modules:
  0.0 67.4 jit_solution(11842907657280808292)
XLA Ops:
  1.3 63.2 %shard_map.104 = (bf16[16,4096]{1,0:T(8,128)(2,1)}, bf16[4,8,576]{2,1,0:T(8,128)(2,1)}) custom-call(s32[1]{0:T(128)S(6)} %copy.13.len_ref, s32[64]{0:T(128)} %own_ref.1, s32[64]{0:T(128)} %slot_ref.1, bf16[256,512]{1,0:T(8,128)(2,1)} %qn_hbm.1, bf16[256,256]{1,0:T(8,128)(2,1)} %qr_hbm.1, bf16[576,2048]{1,0:T(8,128)(2,1)} %bitcast.2, ...), custom_call_target="tpu_custom_call" | custom-call | flops 5000000000 | bytes 6000000 | tf_op jit(solution)/shard_map/pallas_call | solution.py:361
  64.5 1.6 %copy.14 = bf16[16,4096]{1,0:T(8,128)(2,1)} copy(bf16[16,4096]{1,0:T(8,128)(2,1)} %get-tuple-element.4) | data formatting | bytes 262144
  66.0 1.4 %copy.15 = bf16[4,8,576]{2,1,0:T(8,128)(2,1)} copy(bf16[4,8,576]{2,1,0:T(8,128)(2,1)} %get-tuple-element.5) | data formatting | bytes 73728

commit v3 on v2

v3 whole, which is shorter than its diff:
```python
import jax
import jax.numpy as jnp
from jax import lax
from jax.experimental import pallas as pl
from jax.experimental.pallas import tpu as pltpu
from jax.sharding import PartitionSpec as P

NOPE = 128
ROPE = 64
VDIM = 128
KVR = 512
KVW = 576
SLOTS = 4
SPAN = 256
PREFIX = 2048
KEYS = PREFIX + SPAN
HEADS_DEV = 4
GRP = 32
Z = 16
W_ROWS = 512
NL_ROWS = 80
BLK_ROWS = W_ROWS + NL_ROWS
PIECES = ((0, 160), (160, 144), (304, 144), (448, 144))
STEPS = range(9)
NEAR = range(7)
FAR = (7, 8)
MESH = pl.DeviceIdType.MESH
F32 = jnp.float32
BF16 = jnp.bfloat16


def kernel(
    len_ref, own_ref, slot_ref, qn_hbm, qr_hbm, cache_hbm, nl_hbm, up_hbm, w_hbm,
    mixed_ref, dec_ref,
    qn, qr, cache, up, nl, fresh, up_t, kv, ropes, ring, att, part1, part2, p1, mid1, mid2, p2_1, p2_2, p1_1,
    direct1, direct2, res1, res2, res_in1, res_in2, dec, dec_in,
    in_sem, ring_send, ring_recv, first_sem, nl_sem, att_sem, sums_send, p1_recv, p2_recv, direct_recv, res_recv,
    dec_sem,
):
    g = lax.axis_index("grp")
    t = lax.axis_index("tp")
    z, core = g // 2, lax.rem(g, 2)
    x, y = t // 4, lax.rem(t, 4)
    ahead = 1 - 2 * core
    ring_to = {"grp": lax.rem(g + 2 * ahead + GRP, GRP)}
    ring_from = {"grp": lax.rem(g - 2 * ahead + GRP, GRP)}
    sibling = {"grp": g + 1 - 2 * core}
    xs = [lax.rem(x + d, 4) for d in (1, 2, 3)]
    ys = [lax.rem(y + d, 4) for d in (1, 2, 3)]
    x_peers = [{"tp": xx * 4 + y} for xx in xs]
    y_peers = [{"tp": x * 4 + yy} for yy in ys]

    plane = [(dx, dy) for dx in range(4) for dy in range(4)][1:]
    plane_xy = [(lax.rem(x + dx, 4), lax.rem(y + dy, 4)) for dx, dy in plane]
    plane_peers = [{"tp": xx * 4 + yy} for xx, yy in plane_xy]
    partners = [ring_from, ring_to, sibling] + plane_peers
    barrier = pltpu.get_barrier_semaphore()
    for who in partners:
        pl.semaphore_signal(barrier, inc=1, device_id=who, device_id_type=MESH)

    loads = [
        pltpu.make_async_copy(nl_hbm, nl, in_sem.at[0]),
        pltpu.make_async_copy(w_hbm, ring.at[0, pl.ds(0, W_ROWS)], in_sem.at[1]),
        pltpu.make_async_copy(up_hbm, up, in_sem.at[2]),
        pltpu.make_async_copy(cache_hbm, cache, in_sem.at[3]),
        pltpu.make_async_copy(qn_hbm, qn, in_sem.at[4]),
        pltpu.make_async_copy(qr_hbm, qr, in_sem.at[5]),
    ]
    for load in loads:
        load.start()
    loads[0].wait()
    rows = nl[...]
    tiles = [rows[:, k * 128 : (k + 1) * 128] for k in range(4)]
    tiles.append(jnp.concatenate([rows[:, KVR:], jnp.zeros((16, 64), BF16)], axis=1))
    packed = jnp.concatenate(tiles, axis=0)
    ring[0, pl.ds(W_ROWS, NL_ROWS), :] = packed
    fresh[t] = packed
    loads[1].wait()
    pl.semaphore_wait(barrier, len(partners))

    def remote(src, dst, send, recv, who):
        return pltpu.make_async_remote_copy(
            src_ref=src, dst_ref=dst, send_sem=send, recv_sem=recv, device_id=who, device_id_type=MESH
        )

    def hop(b, k):
        at, n = PIECES[k]
        piece = pl.ds(at, n)
        return remote(ring.at[b, piece], ring.at[b + 2, piece], ring_send.at[0], ring_recv.at[b + 2, k], ring_to)

    coming = [(b, k) for b in range(2, 17) for k in range(len(PIECES))]

    def serve(n):
        for _ in range(n * len(PIECES) // 2):
            b, k = coming.pop(0)
            hop(b - 2, k).wait_recv()
            if b < 15:
                hop(b, k).start()

    first = remote(ring.at[0], ring.at[1], first_sem.at[0], first_sem.at[1], sibling)

    def new_rows(i):
        return remote(fresh.at[t], fresh.at[t], nl_sem.at[0], nl_sem.at[1], plane_peers[i])

    others = fresh.at[pl.ds(0, 15)]
    all_new_rows = remote(others, others, nl_sem.at[0], nl_sem.at[1], plane_peers[0])

    for k in range(len(PIECES)):
        hop(0, k).start()
    first.start()
    for i in range(15):
        new_rows(i).start()

    def look(n, codes):
        u, i = n // 2, lax.rem(n, 2)
        b = jnp.where(u > 0, u + 1, 0)
        plane = lax.rem(z - ahead * (b // 2) + Z, Z)
        block = 2 * (2 * plane + lax.rem(core + b, 2)) + i
        owner, place = own_ref[block], slot_ref[block]
        wanted = [(who, s) for who in (g, g + 1 - 2 * core) for s in range(SLOTS)]
        return tuple(
            jnp.where(jnp.logical_and(owner == who, place == s), 2 * b + i, old)
            for (who, s), old in zip(wanted, codes, strict=True)
        )

    codes = lax.fori_loop(0, 2 * Z, look, (jnp.int32(-1),) * (2 * SLOTS))

    def rope_rows(rope, at, n):
        zero = jnp.zeros((64, n), BF16)
        ropes[0, :, pl.ds(at, n)] = jnp.concatenate([rope, zero], axis=0)
        ropes[1, :, pl.ds(at, n)] = jnp.concatenate([zero, rope], axis=0)

    for i in (2, 3):
        loads[i].wait()

    up_t[...] = up[...].T

    def prefix_keys(i, _):
        at = pl.multiple_of(i * 256, 256)
        kv[:, pl.ds(at, 256)] = jnp.dot(
            up_t[...], cache[pl.ds(0, KVR), pl.ds(at, 256)], preferred_element_type=F32
        ).astype(BF16)
        rope_rows(cache[pl.ds(KVR, ROPE), pl.ds(at, 256)], at, 256)
        return _

    lax.fori_loop(0, 2, prefix_keys, 0)
    first.wait_recv()
    for k in range(len(PIECES)):
        hop(1, k).start()
    lax.fori_loop(2, 5, prefix_keys, 0)
    serve(1)
    lax.fori_loop(5, 8, prefix_keys, 0)
    serve(2)
    all_new_rows.wait_recv()
    new = fresh[...].reshape(16, 5, 16, 128)
    new = [new[:, k].reshape(SPAN, 128) for k in range(5)]
    kv[:, pl.ds(PREFIX, SPAN)] = lax.dot_general(
        up_t[...], jnp.concatenate(new[:4], axis=1), (((1,), (1,)), ((), ())), preferred_element_type=F32
    ).astype(BF16)
    rope_rows(new[4].T[:ROPE], PREFIX, SPAN)

    for i in (4, 5):
        loads[i].wait()
    to_bits = (NOPE + ROPE) ** -0.5 * 1.4426950408889634
    col = lax.broadcasted_iota(jnp.int32, (1, PREFIX), 1)
    old_bias = jnp.where(col < len_ref[0], 0.0, -1e30).astype(F32)
    row = lax.broadcasted_iota(jnp.int32, (SPAN, SPAN), 0)
    key = lax.broadcasted_iota(jnp.int32, (SPAN, SPAN), 1)
    token = ((key // 8) % 2) * 128 + (key // 16) * 8 + key % 8
    new_bias = jnp.where(token <= row, 0.0, -1e30).astype(F32)

    ones = jnp.ones((VDIM, KEYS), BF16)

    def weights(h):
        k = jnp.concatenate([kv[h * 256 : h * 256 + NOPE], ropes[h % 2]], axis=0)
        pair = h // 2
        q = jnp.concatenate([qn[:, h * 128 : (h + 1) * 128], qr[:, pair * 128 : (pair + 1) * 128]], axis=1)
        s = jnp.dot((q.astype(F32) * to_bits).astype(BF16), k, preferred_element_type=F32)
        s = jnp.concatenate([s[:, :PREFIX] + old_bias, s[:, PREFIX:] + new_bias], axis=1)
        return jnp.exp2(s - jnp.max(s, axis=1, keepdims=True)).astype(BF16)

    def attend(h, e):
        v = jnp.concatenate([kv[h * 256 + NOPE : (h + 1) * 256], ones], axis=0)
        o = lax.dot_general(e, v, (((1,), (1,)), ((), ())), preferred_element_type=F32)
        att[0, :, h * 128 : (h + 1) * 128] = (o[:, :VDIM] / o[:, VDIM:]).astype(BF16)

    def swap(h):
        cols = pl.ds(h * 128, 128)
        return remote(att.at[0, :, cols], att.at[1, :, cols], att_sem.at[0, h], att_sem.at[1, h], sibling)

    serve(2)
    e = weights(0)
    for h in range(1, HEADS_DEV):
        serve(1)
        attend(h - 1, e)
        e = weights(h)
        swap(h - 1).start()
        serve(1)
    attend(HEADS_DEV - 1, e)
    swap(HEADS_DEV - 1).start()
    serve(1)

    def wide(s):
        return 1 <= s <= 7

    def part(s, *at):
        return part2.at[(s - 1, *at)] if wide(s) else part1.at[(s // 8, *at)]

    def mid(s, *at):
        return mid2.at[(s - 1, *at)] if wide(s) else mid1.at[at]

    def first_in(s, *at):
        return p1.at[(s - 1, *at)] if wide(s) else p1_1.at[at]

    def second_in(s, *at):
        return p2_2.at[(s - 1, *at)] if wide(s) else p2_1.at[at]

    def direct_in(s, *at):
        return direct2.at[at] if wide(s) else direct1.at[at]

    def res(s):
        return res2.at[s - 1] if wide(s) else res1.at[s // 8]

    def res_in(s):
        return res_in2.at[s - 1] if wide(s) else res_in1.at[s // 8]

    def out_first(s, i):
        src = part(s, slice(None), slice(None), ys[i]) if s % 2 else part(s, slice(None), xs[i])
        who = y_peers[i] if s % 2 else x_peers[i]
        return remote(src, first_in(s, i), sums_send.at[int(wide(s))], p1_recv.at[s], who)

    def out_second(s, i):
        src = mid(s, slice(None), xs[i] if s % 2 else ys[i])
        who = x_peers[i] if s % 2 else y_peers[i]
        return remote(src, second_in(s, i), sums_send.at[2 + int(wide(s))], p2_recv.at[s], who)

    def out_direct(s, i):
        xx, yy = plane_xy[i]
        src = part(s, slice(None), xx, yy)
        return remote(src, direct_in(s, i), sums_send.at[4 + int(wide(s))], direct_recv.at[int(wide(s))], plane_peers[i])

    def out_res(s):
        return remote(res(s), res_in(s), sums_send.at[6 + int(wide(s))], res_recv.at[s], sibling)

    def arrived(ref, sem):
        remote(ref, ref, sem, sem, sibling).wait_recv()

    def left(ref, sem):
        remote(ref, ref, sem, sem, sibling).wait_send()

    def project(s):
        w = [ring[b, pl.ds(0, W_ROWS), :] for b in ((2 * s, 2 * s + 1) if wide(s) else (2 * s,))]
        a = att[...].reshape(2 * SPAN, W_ROWS)
        o = jnp.dot(a, jnp.concatenate(w, axis=1), preferred_element_type=F32).astype(BF16)
        part(s)[...] = o.reshape(2, 4, 4, 16, 128 * len(w))
        for i in range(15 if s in FAR else 3):
            (out_direct if s in FAR else out_first)(s, i).start()

    def add(own, terms):
        total = own[...].astype(F32)
        for term in terms:
            total += term[...].astype(F32)
        return total.astype(BF16)

    def first_sum(s):
        arrived(first_in(s), p1_recv.at[s])
        own = part(s, slice(None), slice(None), y) if s % 2 else part(s, slice(None), x)
        mid(s)[...] = add(own, [first_in(s, i) for i in range(3)])
        for i in range(3):
            out_second(s, i).start()

    def store(s, rows, core, ahead):
        plane = lax.rem(z - ahead * s + Z, Z)
        for n in range(2 if wide(s) else 1):
            at = pl.multiple_of((2 * plane + lax.rem(core + n, 2)) * 128, 128)
            mixed_ref[:, pl.ds(at, 128)] = rows[:, n * 128 : (n + 1) * 128]

    def deliver(s, total):
        res(s)[...] = total[1]
        out_res(s).start()
        store(s, total[0], core, ahead)

    def second_sum(s):
        arrived(second_in(s), p2_recv.at[s])
        own = mid(s, slice(None), x if s % 2 else y)
        deliver(s, add(own, [second_in(s, i) for i in range(3)]))

    def direct_sum(s):
        arrived(direct_in(s), direct_recv.at[int(wide(s))])
        deliver(s, add(part(s, slice(None), x, y), [direct_in(s, i) for i in range(15)]))

    def collect(s):
        arrived(res_in(s), res_recv.at[s])
        store(s, res_in(s)[...], 1 - core, -ahead)

    for h in range(HEADS_DEV):
        swap(h).wait_recv()
    serve(1)
    project(0)
    project(1)
    serve(1)
    project(2)
    project(3)
    serve(2)
    project(4)
    serve(2)
    first_sum(0)
    serve(1)
    first_sum(1)
    serve(1)
    project(5)
    serve(1)
    first_sum(2)
    serve(1)
    first_sum(3)
    serve(2)
    project(6)
    first_sum(4)
    second_sum(0)
    serve(1)
    second_sum(1)
    second_sum(2)
    serve(1)
    first_sum(5)
    serve(1)
    second_sum(3)
    serve(1)
    project(7)
    second_sum(4)
    serve(2)
    project(8)
    first_sum(6)
    second_sum(5)
    assert not coming

    def pick(code):
        got = ring[jnp.maximum(code, 0) // 2, pl.ds(W_ROWS, NL_ROWS), :].reshape(5, 16, 128).astype(F32)
        got = jnp.where(lax.rem(jnp.maximum(code, 0), 2) == 0, got[:, :8], got[:, 8:])
        got = jnp.where(code >= 0, got, 0.0)
        return jnp.concatenate([got[k] for k in range(5)], axis=1)

    for s in range(0, SLOTS, 2):
        both = jnp.concatenate([pick(codes[SLOTS + s]), pick(codes[SLOTS + s + 1])], axis=0)
        dec[s // 2] = both.astype(BF16)
    swap_dec = remote(dec, dec_in, dec_sem.at[0], dec_sem.at[1], sibling)
    swap_dec.start()
    mine = [pick(codes[s]) for s in range(SLOTS)]
    swap_dec.wait_recv()
    for s in range(SLOTS):
        other = dec_in[s // 2].astype(F32)[(s % 2) * 8 : (s % 2) * 8 + 8]
        dec_ref[s] = (mine[s] + other)[:, :KVW].astype(BF16)

    for s in (0, 1, 2, 3, 4, 5):
        collect(s)
    direct_sum(7)
    second_sum(6)
    collect(7)
    collect(6)
    direct_sum(8)
    collect(8)

    left(ring.at[pl.ds(2, 15)], ring_send.at[0])
    first.wait_send()
    all_new_rows.wait_send()
    for h in range(HEADS_DEV):
        swap(h).wait_send()
    swap_dec.wait_send()
    for n, ref in enumerate((p1_1, p1, p2_1, p2_2, direct1, direct2, res_in1, res_in2)):
        left(ref, sums_send.at[n])


def body(query_nope, query_rope, latent_cache, new_latent, prefix_length, latent_up, out_proj, owners, slot_index):
    nl = new_latent.reshape(16, KVW)
    cache = latent_cache.T
    smem = pl.BlockSpec(memory_space=pltpu.SMEM)
    hbm = pl.BlockSpec(memory_space=pl.ANY)
    vmem = pl.BlockSpec(memory_space=pltpu.VMEM)
    dma = pltpu.SemaphoreType.DMA
    nk = len(PIECES)
    return pl.pallas_call(
        kernel,
        out_shape=(
            jax.ShapeDtypeStruct((16, 4096), BF16),
            jax.ShapeDtypeStruct((SLOTS, 8, KVW), BF16),
        ),
        in_specs=[smem] * 3 + [hbm] * 6,
        out_specs=(vmem, vmem),
        scratch_shapes=[
            pltpu.VMEM((SPAN, 512), BF16),
            pltpu.VMEM((SPAN, 256), BF16),
            pltpu.VMEM((KVW, PREFIX), BF16),
            pltpu.VMEM((KVR, 1024), BF16),
            pltpu.VMEM((16, KVW), BF16),
            pltpu.VMEM((16, NL_ROWS, 128), BF16),
            pltpu.VMEM((1024, KVR), BF16),
            pltpu.VMEM((1024, KEYS), BF16),
            pltpu.VMEM((2, 128, KEYS), BF16),
            pltpu.VMEM((17, BLK_ROWS, 128), BF16),
            pltpu.VMEM((2, SPAN, 512), BF16),
            pltpu.VMEM((2, 2, 4, 4, 16, 128), BF16),
            pltpu.VMEM((7, 2, 4, 4, 16, 256), BF16),
            pltpu.VMEM((6, 3, 2, 4, 16, 256), BF16),
            pltpu.VMEM((2, 4, 16, 128), BF16),
            pltpu.VMEM((6, 2, 4, 16, 256), BF16),
            pltpu.VMEM((3, 2, 16, 128), BF16),
            pltpu.VMEM((6, 3, 2, 16, 256), BF16),
            pltpu.VMEM((3, 2, 4, 16, 128), BF16),
            pltpu.VMEM((15, 2, 16, 128), BF16),
            pltpu.VMEM((15, 2, 16, 256), BF16),
            pltpu.VMEM((2, 16, 128), BF16),
            pltpu.VMEM((7, 16, 256), BF16),
            pltpu.VMEM((2, 16, 128), BF16),
            pltpu.VMEM((7, 16, 256), BF16),
            pltpu.VMEM((2, 16, 640), BF16),
            pltpu.VMEM((2, 16, 640), BF16),
            dma((6,)),
            dma((1,)),
            dma((17, nk)),
            dma((2,)),
            dma((2,)),
            dma((2, HEADS_DEV)),
            dma((8,)),
            dma((7,)),
            dma((7,)),
            dma((2,)),
            dma((9,)),
            dma((2,)),
        ],
        compiler_params=pltpu.CompilerParams(
            collective_id=0, has_side_effects=True, vmem_limit_bytes=56 * 1024 * 1024
        ),
        cost_estimate=pl.CostEstimate(flops=5_000_000_000, bytes_accessed=6_000_000, transcendentals=2_400_000),
    )(prefix_length, owners, slot_index, query_nope, query_rope, cache, nl, latent_up, out_proj)


def solution(mesh):
    placed = (
        P("grp", "tp"),
        P("grp", "tp"),
        P("grp", None),
        P("grp", "tp", None),
        P("grp"),
        P(None, "tp"),
        P("tp", "grp"),
        P(),
        P(),
    )
    return jax.shard_map(
        body,
        mesh=mesh,
        in_specs=placed,
        out_specs=(P(("grp", "tp"), None), P("grp", "tp", None)),
        check_vma=False,
    )
```

time: 67.7 us -> 61.5 us (0.908)
  Pallas kernels: 63.2 us -> 57 us
    pallas_call x1, Pallas kernels: 63.2 us -> 57 us  [body(): pl.pallas_call(kernel, out_shape=(jax.ShapeDtypeStruct((16, 4096), BF16),...]
where the time goes in v3:
time: 61.5 us; the launch traced here: 61.3 us
  Pallas kernels  57 us (93%)
  local copies, waits for them, and re-layouts  2.97 us (5%)
  between operations  1.29 us (2%)
    pallas_call x1, Pallas kernels, body(): pl.pallas_call(kernel, out_shape=(jax.ShapeDtypeStruct((16, 4096), BF16),...  57 us
    unnamed x2, local copies, waits for them, and re-layouts  2.97 us

profile of v3, /device:TPU:1, one launch (start us, length us, event | category | flops | bytes accessed | tf_op | source)
XLA Modules:
  0.0 61.3 jit_solution(4125080876726311568)
XLA Ops:
  1.3 57.0 %shard_map.104 = (bf16[16,4096]{1,0:T(8,128)(2,1)}, bf16[4,8,576]{2,1,0:T(8,128)(2,1)}) custom-call(s32[1]{0:T(128)S(6)} %copy.13.len_ref, s32[64]{0:T(128)} %own_ref.1, s32[64]{0:T(128)} %slot_ref.1, bf16[256,512]{1,0:T(8,128)(2,1)} %qn_hbm.1, bf16[256,256]{1,0:T(8,128)(2,1)} %qr_hbm.1, bf16[576,2048]{1,0:T(8,128)(2,1)} %bitcast.2, ...), custom_call_target="tpu_custom_call" | custom-call | flops 5000000000 | bytes 6000000 | tf_op jit(solution)/shard_map/pallas_call | solution.py:380
  58.3 1.6 %copy.14 = bf16[16,4096]{1,0:T(8,128)(2,1)} copy(bf16[16,4096]{1,0:T(8,128)(2,1)} %get-tuple-element.4) | data formatting | bytes 262144
  59.9 1.4 %copy.15 = bf16[4,8,576]{2,1,0:T(8,128)(2,1)} copy(bf16[4,8,576]{2,1,0:T(8,128)(2,1)} %get-tuple-element.5) | data formatting | bytes 73728

commit v4 on v3

--- a/solution.py
+++ b/solution.py
@@ -20,10 +20,9 @@
 W_ROWS = 512
 NL_ROWS = 80
 BLK_ROWS = W_ROWS + NL_ROWS
-PIECES = ((0, 160), (160, 144), (304, 144), (448, 144))
-STEPS = range(9)
+PIECES = ((0, 304), (304, 288))
 NEAR = range(7)
-FAR = (7, 8)
+FAR = (14, 15, 16)
 MESH = pl.DeviceIdType.MESH
 F32 = jnp.float32
 BF16 = jnp.bfloat16
@@ -32,9 +31,9 @@
 def kernel(
     len_ref, own_ref, slot_ref, qn_hbm, qr_hbm, cache_hbm, nl_hbm, up_hbm, w_hbm,
     mixed_ref, dec_ref,
-    qn, qr, cache, up, nl, fresh, up_t, kv, ropes, ring, att, part1, part2, p1, mid1, mid2, p2_1, p2_2, p1_1,
-    direct1, direct2, res1, res2, res_in1, res_in2, dec, dec_in,
-    in_sem, ring_send, ring_recv, first_sem, nl_sem, att_sem, sums_send, p1_recv, p2_recv, direct_recv, res_recv,
+    qn, qr, cache, up, nl, fresh, up_t, kv, ropes, ring, att, part1, part2, p1_1, p1_2, mid1, mid2, p2_1, p2_2,
+    res1, res2, res_in1, res_in2, part_far, direct, res_far, res_in_far, dec, dec_in,
+    in_sem, ring_send, ring_recv, first_sem, nl_sem, att_sem, sums_send, p1_recv, p2_recv, res_recv, far_send, far_recv,
     dec_sem,
 ):
     g = lax.axis_index("grp")
@@ -45,12 +44,13 @@
     ring_to = {"grp": lax.rem(g + 2 * ahead + GRP, GRP)}
     ring_from = {"grp": lax.rem(g - 2 * ahead + GRP, GRP)}
     sibling = {"grp": g + 1 - 2 * core}
-    xs = [lax.rem(x + d, 4) for d in (1, 2, 3)]
-    ys = [lax.rem(y + d, 4) for d in (1, 2, 3)]
+    xs = [lax.rem(x + d, 4) for d in (2, 1, 3)]
+    ys = [lax.rem(y + d, 4) for d in (2, 1, 3)]
     x_peers = [{"tp": xx * 4 + y} for xx in xs]
     y_peers = [{"tp": x * 4 + yy} for yy in ys]
 
     plane = [(dx, dy) for dx in range(4) for dy in range(4)][1:]
+    plane.sort(key=lambda d: -min(d[0], 4 - d[0]) - min(d[1], 4 - d[1]))
     plane_xy = [(lax.rem(x + dx, 4), lax.rem(y + dy, 4)) for dx, dy in plane]
     plane_peers = [{"tp": xx * 4 + yy} for xx, yy in plane_xy]
     partners = [ring_from, ring_to, sibling] + plane_peers
@@ -200,47 +200,43 @@
     swap(HEADS_DEV - 1).start()
     serve(1)
 
-    def wide(s):
-        return 1 <= s <= 7
-
     def part(s, *at):
-        return part2.at[(s - 1, *at)] if wide(s) else part1.at[(s // 8, *at)]
+        return part2.at[(s - 1, *at)] if s else part1.at[at]
 
     def mid(s, *at):
-        return mid2.at[(s - 1, *at)] if wide(s) else mid1.at[at]
+        return mid2.at[(s - 1, *at)] if s else mid1.at[at]
 
     def first_in(s, *at):
-        return p1.at[(s - 1, *at)] if wide(s) else p1_1.at[at]
+        return p1_2.at[(s - 1, *at)] if s else p1_1.at[at]
 
     def second_in(s, *at):
-        return p2_2.at[(s - 1, *at)] if wide(s) else p2_1.at[at]
-
-    def direct_in(s, *at):
-        return direct2.at[at] if wide(s) else direct1.at[at]
+        return p2_2.at[(s - 1, *at)] if s else p2_1.at[at]
 
     def res(s):
-        return res2.at[s - 1] if wide(s) else res1.at[s // 8]
+        return res2.at[s - 1] if s else res1
 
     def res_in(s):
-        return res_in2.at[s - 1] if wide(s) else res_in1.at[s // 8]
+        return res_in2.at[s - 1] if s else res_in1
 
     def out_first(s, i):
         src = part(s, slice(None), slice(None), ys[i]) if s % 2 else part(s, slice(None), xs[i])
         who = y_peers[i] if s % 2 else x_peers[i]
-        return remote(src, first_in(s, i), sums_send.at[int(wide(s))], p1_recv.at[s], who)
+        return remote(src, first_in(s, i), sums_send.at[int(s > 0)], p1_recv.at[s], who)
 
     def out_second(s, i):
         src = mid(s, slice(None), xs[i] if s % 2 else ys[i])
         who = x_peers[i] if s % 2 else y_peers[i]
-        return remote(src, second_in(s, i), sums_send.at[2 + int(wide(s))], p2_recv.at[s], who)
-
-    def out_direct(s, i):
+        return remote(src, second_in(s, i), sums_send.at[2 + int(s > 0)], p2_recv.at[s], who)
+
+    def out_res(s):
+        return remote(res(s), res_in(s), sums_send.at[4 + int(s > 0)], res_recv.at[s], sibling)
+
+    def out_far(f, i):
         xx, yy = plane_xy[i]
-        src = part(s, slice(None), xx, yy)
-        return remote(src, direct_in(s, i), sums_send.at[4 + int(wide(s))], direct_recv.at[int(wide(s))], plane_peers[i])
-
-    def out_res(s):
-        return remote(res(s), res_in(s), sums_send.at[6 + int(wide(s))], res_recv.at[s], sibling)
+        return remote(part_far.at[f, :, xx, yy], direct.at[f, i], far_send.at[0, f], far_recv.at[0, f], plane_peers[i])
+
+    def out_res_far(f):
+        return remote(res_far.at[f], res_in_far.at[f], far_send.at[1, f], far_recv.at[1, f], sibling)
 
     def arrived(ref, sem):
         remote(ref, ref, sem, sem, sibling).wait_recv()
@@ -248,13 +244,21 @@
     def left(ref, sem):
         remote(ref, ref, sem, sem, sibling).wait_send()
 
-    def project(s):
-        w = [ring[b, pl.ds(0, W_ROWS), :] for b in ((2 * s, 2 * s + 1) if wide(s) else (2 * s,))]
+    def times(blocks):
+        w = [ring[b, pl.ds(0, W_ROWS), :] for b in blocks]
         a = att[...].reshape(2 * SPAN, W_ROWS)
         o = jnp.dot(a, jnp.concatenate(w, axis=1), preferred_element_type=F32).astype(BF16)
-        part(s)[...] = o.reshape(2, 4, 4, 16, 128 * len(w))
-        for i in range(15 if s in FAR else 3):
-            (out_direct if s in FAR else out_first)(s, i).start()
+        return o.reshape(2, 4, 4, 16, 128 * len(w))
+
+    def project(s):
+        part(s)[...] = times((2 * s, 2 * s + 1) if s else (0,))
+        for i in range(3):
+            out_first(s, i).start()
+
+    def project_far(f):
+        part_far[f] = times((FAR[f],))
+        for i in range(15):
+            out_far(f, i).start()
 
     def add(own, terms):
         total = own[...].astype(F32)
@@ -269,29 +273,34 @@
         for i in range(3):
             out_second(s, i).start()
 
-    def store(s, rows, core, ahead):
-        plane = lax.rem(z - ahead * s + Z, Z)
-        for n in range(2 if wide(s) else 1):
-            at = pl.multiple_of((2 * plane + lax.rem(core + n, 2)) * 128, 128)
+    def store(b, rows, core, ahead):
+        plane = lax.rem(z - ahead * (b // 2) + Z, Z)
+        for n in range(rows.shape[1] // 128):
+            at = pl.multiple_of((2 * plane + lax.rem(core + b + n, 2)) * 128, 128)
             mixed_ref[:, pl.ds(at, 128)] = rows[:, n * 128 : (n + 1) * 128]
-
-    def deliver(s, total):
-        res(s)[...] = total[1]
-        out_res(s).start()
-        store(s, total[0], core, ahead)
 
     def second_sum(s):
         arrived(second_in(s), p2_recv.at[s])
         own = mid(s, slice(None), x if s % 2 else y)
-        deliver(s, add(own, [second_in(s, i) for i in range(3)]))
-
-    def direct_sum(s):
-        arrived(direct_in(s), direct_recv.at[int(wide(s))])
-        deliver(s, add(part(s, slice(None), x, y), [direct_in(s, i) for i in range(15)]))
+        total = add(own, [second_in(s, i) for i in range(3)])
+        res(s)[...] = total[1]
+        out_res(s).start()
+        store(2 * s, total[0], core, ahead)
+
+    def direct_sum(f):
+        arrived(direct.at[f], far_recv.at[0, f])
+        total = add(part_far.at[f, :, x, y], [direct.at[f, i] for i in range(15)])
+        res_far[f] = total[1]
+        out_res_far(f).start()
+        store(FAR[f], total[0], core, ahead)
 
     def collect(s):
         arrived(res_in(s), res_recv.at[s])
-        store(s, res_in(s)[...], 1 - core, -ahead)
+        store(2 * s, res_in(s)[...], 1 - core, -ahead)
+
+    def collect_far(f):
+        arrived(res_in_far.at[f], far_recv.at[1, f])
+        store(FAR[f], res_in_far[f], 1 - core, -ahead)
 
     for h in range(HEADS_DEV):
         swap(h).wait_recv()
@@ -321,15 +330,15 @@
     second_sum(1)
     second_sum(2)
     serve(1)
+    project_far(0)
     first_sum(5)
-    serve(1)
     second_sum(3)
-    serve(1)
-    project(7)
+    serve(2)
+    project_far(1)
+    first_sum(6)
     second_sum(4)
     serve(2)
-    project(8)
-    first_sum(6)
+    project_far(2)
     second_sum(5)
     assert not coming
 
@@ -350,23 +359,28 @@
         other = dec_in[s // 2].astype(F32)[(s % 2) * 8 : (s % 2) * 8 + 8]
         dec_ref[s] = (mine[s] + other)[:, :KVW].astype(BF16)
 
-    for s in (0, 1, 2, 3, 4, 5):
+    for s in range(6):
         collect(s)
-    direct_sum(7)
+    direct_sum(0)
+    direct_sum(1)
     second_sum(6)
-    collect(7)
+    collect_far(0)
+    collect_far(1)
     collect(6)
-    direct_sum(8)
-    collect(8)
-
     left(ring.at[pl.ds(2, 15)], ring_send.at[0])
     first.wait_send()
     all_new_rows.wait_send()
     for h in range(HEADS_DEV):
         swap(h).wait_send()
     swap_dec.wait_send()
-    for n, ref in enumerate((p1_1, p1, p2_1, p2_2, direct1, direct2, res_in1, res_in2)):
+    for n, ref in enumerate((p1_1, p1_2, p2_1, p2_2, res_in1, res_in2)):
         left(ref, sums_send.at[n])
+    for f in range(3):
+        left(direct.at[f], far_send.at[0, f])
+    direct_sum(2)
+    collect_far(2)
+    for f in range(3):
+        left(res_in_far.at[f], far_send.at[1, f])
 
 
 def body(query_nope, query_rope, latent_cache, new_latent, prefix_length, latent_up, out_proj, owners, slot_index):
@@ -380,8 +394,8 @@
     return pl.pallas_call(
         kernel,
         out_shape=(
-            jax.ShapeDtypeStruct((16, 4096), BF16),
-            jax.ShapeDtypeStruct((SLOTS, 8, KVW), BF16),
+            pltpu.VMEM((16, 4096), BF16),
+            pltpu.VMEM((SLOTS, 8, KVW), BF16),
         ),
         in_specs=[smem] * 3 + [hbm] * 6,
         out_specs=(vmem, vmem),
@@ -397,20 +411,22 @@
             pltpu.VMEM((2, 128, KEYS), BF16),
             pltpu.VMEM((17, BLK_ROWS, 128), BF16),
             pltpu.VMEM((2, SPAN, 512), BF16),
-            pltpu.VMEM((2, 2, 4, 4, 16, 128), BF16),
-            pltpu.VMEM((7, 2, 4, 4, 16, 256), BF16),
+            pltpu.VMEM((2, 4, 4, 16, 128), BF16),
+            pltpu.VMEM((6, 2, 4, 4, 16, 256), BF16),
+            pltpu.VMEM((3, 2, 4, 16, 128), BF16),
             pltpu.VMEM((6, 3, 2, 4, 16, 256), BF16),
             pltpu.VMEM((2, 4, 16, 128), BF16),
             pltpu.VMEM((6, 2, 4, 16, 256), BF16),
             pltpu.VMEM((3, 2, 16, 128), BF16),
             pltpu.VMEM((6, 3, 2, 16, 256), BF16),
-            pltpu.VMEM((3, 2, 4, 16, 128), BF16),
-            pltpu.VMEM((15, 2, 16, 128), BF16),
-            pltpu.VMEM((15, 2, 16, 256), BF16),
-            pltpu.VMEM((2, 16, 128), BF16),
-            pltpu.VMEM((7, 16, 256), BF16),
-            pltpu.VMEM((2, 16, 128), BF16),
-            pltpu.VMEM((7, 16, 256), BF16),
+            pltpu.VMEM((16, 128), BF16),
+            pltpu.VMEM((6, 16, 256), BF16),
+            pltpu.VMEM((16, 128), BF16),
+            pltpu.VMEM((6, 16, 256), BF16),
+            pltpu.VMEM((3, 2, 4, 4, 16, 128), BF16),
+            pltpu.VMEM((3, 15, 2, 16, 128), BF16),
+            pltpu.VMEM((3, 16, 128), BF16),
+            pltpu.VMEM((3, 16, 128), BF16),
             pltpu.VMEM((2, 16, 640), BF16),
             pltpu.VMEM((2, 16, 640), BF16),
             dma((6,)),
@@ -419,11 +435,12 @@
             dma((2,)),
             dma((2,)),
             dma((2, HEADS_DEV)),
-            dma((8,)),
+            dma((6,)),
             dma((7,)),
             dma((7,)),
-            dma((2,)),
-            dma((9,)),
+            dma((7,)),
+            dma((2, 3)),
+            dma((2, 3)),
             dma((2,)),
         ],
         compiler_params=pltpu.CompilerParams(

time: 61.5 us -> 57.6 us (0.937)
  Pallas kernels: 57 us -> 54.9 us
  local copies, waits for them, and re-layouts: 2.97 us -> 1.27 us
    pallas_call x1, Pallas kernels: 57 us -> 54.9 us  [body(): pl.pallas_call(kernel, out_shape=(pltpu.VMEM((16, 4096), BF16), pltpu.VME...]
    unnamed x2, local copies, waits for them, and re-layouts: 2.97 us -> 1.27 us
where the time goes in v4:
time: 57.6 us; the launch traced here: 57.5 us
  Pallas kernels  54.9 us (95%)
  between operations  1.29 us (2%)
  local copies, waits for them, and re-layouts  1.27 us (2%)
    pallas_call x1, Pallas kernels, body(): pl.pallas_call(kernel, out_shape=(pltpu.VMEM((16, 4096), BF16), pltpu.VME...  54.9 us
    unnamed x2, local copies, waits for them, and re-layouts  1.27 us

profile of v4, /device:TPU:1, one launch (start us, length us, event | category | flops | bytes accessed | tf_op | source)
XLA Modules:
  0.0 57.5 jit_solution(7695169248763748204)
XLA Ops:
  1.3 54.9 %shard_map.104 = (bf16[16,4096]{1,0:T(8,128)(2,1)S(1)}, bf16[4,8,576]{2,1,0:T(8,128)(2,1)S(1)}) custom-call(s32[1]{0:T(128)S(6)} %copy.15.len_ref, s32[64]{0:T(128)} %own_ref.1, s32[64]{0:T(128)} %slot_ref.1, bf16[256,512]{1,0:T(8,128)(2,1)} %qn_hbm.1, bf16[256,256]{1,0:T(8,128)(2,1)} %qr_hbm.1, bf16[576,2048]{1,0:T(8,128)(2,1)} %bitcast.2, ...), custom_call_target="tpu_custom_call" | custom-call | flops 5000000000 | bytes 6000000 | tf_op jit(solution)/shard_map/pallas_call | solution.py:394
  56.2 0.7 %copy.13 = bf16[16,4096]{1,0:T(8,128)(2,1)} copy(bf16[16,4096]{1,0:T(8,128)(2,1)S(1)} %get-tuple-element.2) | data formatting | bytes 262144
  56.9 0.6 %copy.14 = bf16[4,8,576]{2,1,0:T(8,128)(2,1)} copy(bf16[4,8,576]{2,1,0:T(8,128)(2,1)S(1)} %get-tuple-element.3) | data formatting | bytes 73728

commit v5 on v4

--- a/solution.py
+++ b/solution.py
@@ -29,9 +29,9 @@
 
 
 def kernel(
-    len_ref, own_ref, slot_ref, qn_hbm, qr_hbm, cache_hbm, nl_hbm, up_hbm, w_hbm,
+    len_hbm, own_hbm, slot_hbm, qn_hbm, qr_hbm, cache_hbm, nl_hbm, up_hbm, w_hbm,
     mixed_ref, dec_ref,
-    qn, qr, cache, up, nl, fresh, up_t, kv, ropes, ring, att, part1, part2, p1_1, p1_2, mid1, mid2, p2_1, p2_2,
+    len_ref, own_ref, slot_ref, qn, qr, cache, up, nl, fresh, up_t, kv, ropes, ring, att, part1, part2, p1_1, p1_2, mid1, mid2, p2_1, p2_2,
     res1, res2, res_in1, res_in2, part_far, direct, res_far, res_in_far, dec, dec_in,
     in_sem, ring_send, ring_recv, first_sem, nl_sem, att_sem, sums_send, p1_recv, p2_recv, res_recv, far_send, far_recv,
     dec_sem,
@@ -53,10 +53,7 @@
     plane.sort(key=lambda d: -min(d[0], 4 - d[0]) - min(d[1], 4 - d[1]))
     plane_xy = [(lax.rem(x + dx, 4), lax.rem(y + dy, 4)) for dx, dy in plane]
     plane_peers = [{"tp": xx * 4 + yy} for xx, yy in plane_xy]
-    partners = [ring_from, ring_to, sibling] + plane_peers
-    barrier = pltpu.get_barrier_semaphore()
-    for who in partners:
-        pl.semaphore_signal(barrier, inc=1, device_id=who, device_id_type=MESH)
+    partners = plane_peers + [ring_from, ring_to, sibling]
 
     loads = [
         pltpu.make_async_copy(nl_hbm, nl, in_sem.at[0]),
@@ -65,9 +62,31 @@
         pltpu.make_async_copy(cache_hbm, cache, in_sem.at[3]),
         pltpu.make_async_copy(qn_hbm, qn, in_sem.at[4]),
         pltpu.make_async_copy(qr_hbm, qr, in_sem.at[5]),
+        pltpu.make_async_copy(own_hbm, own_ref, in_sem.at[6]),
+        pltpu.make_async_copy(slot_hbm, slot_ref, in_sem.at[7]),
+        pltpu.make_async_copy(len_hbm, len_ref, in_sem.at[8]),
     ]
-    for load in loads:
+    for load in loads[:2]:
         load.start()
+    barrier = pltpu.get_barrier_semaphore()
+    for who in partners:
+        pl.semaphore_signal(barrier, inc=1, device_id=who, device_id_type=MESH)
+    for load in loads[2:]:
+        load.start()
+
+    def rope_rows(rope, at, n):
+        zero = jnp.zeros((64, n), BF16)
+        ropes[0, :, pl.ds(at, n)] = jnp.concatenate([rope, zero], axis=0)
+        ropes[1, :, pl.ds(at, n)] = jnp.concatenate([zero, rope], axis=0)
+
+    def prefix_keys(i, _):
+        at = pl.multiple_of(i * 256, 256)
+        kv[:, pl.ds(at, 256)] = jnp.dot(
+            up_t[...], cache[pl.ds(0, KVR), pl.ds(at, 256)], preferred_element_type=F32
+        ).astype(BF16)
+        rope_rows(cache[pl.ds(KVR, ROPE), pl.ds(at, 256)], at, 256)
+        return _
+
     loads[0].wait()
     rows = nl[...]
     tiles = [rows[:, k * 128 : (k + 1) * 128] for k in range(4)]
@@ -110,6 +129,9 @@
     first.start()
     for i in range(15):
         new_rows(i).start()
+    first.wait_recv()
+    for k in range(len(PIECES)):
+        hop(1, k).start()
 
     def look(n, codes):
         u, i = n // 2, lax.rem(n, 2)
@@ -123,30 +145,11 @@
             for (who, s), old in zip(wanted, codes, strict=True)
         )
 
-    codes = lax.fori_loop(0, 2 * Z, look, (jnp.int32(-1),) * (2 * SLOTS))
-
-    def rope_rows(rope, at, n):
-        zero = jnp.zeros((64, n), BF16)
-        ropes[0, :, pl.ds(at, n)] = jnp.concatenate([rope, zero], axis=0)
-        ropes[1, :, pl.ds(at, n)] = jnp.concatenate([zero, rope], axis=0)
-
-    for i in (2, 3):
-        loads[i].wait()
-
+
+    for load in loads[2:4]:
+        load.wait()
     up_t[...] = up[...].T
-
-    def prefix_keys(i, _):
-        at = pl.multiple_of(i * 256, 256)
-        kv[:, pl.ds(at, 256)] = jnp.dot(
-            up_t[...], cache[pl.ds(0, KVR), pl.ds(at, 256)], preferred_element_type=F32
-        ).astype(BF16)
-        rope_rows(cache[pl.ds(KVR, ROPE), pl.ds(at, 256)], at, 256)
-        return _
-
     lax.fori_loop(0, 2, prefix_keys, 0)
-    first.wait_recv()
-    for k in range(len(PIECES)):
-        hop(1, k).start()
     lax.fori_loop(2, 5, prefix_keys, 0)
     serve(1)
     lax.fori_loop(5, 8, prefix_keys, 0)
@@ -159,7 +162,7 @@
     ).astype(BF16)
     rope_rows(new[4].T[:ROPE], PREFIX, SPAN)
 
-    for i in (4, 5):
+    for i in (4, 5, 8):
         loads[i].wait()
     to_bits = (NOPE + ROPE) ** -0.5 * 1.4426950408889634
     col = lax.broadcasted_iota(jnp.int32, (1, PREFIX), 1)
@@ -312,33 +315,35 @@
     project(3)
     serve(2)
     project(4)
-    serve(2)
+    for load in loads[6:8]:
+        load.wait()
+    codes = lax.fori_loop(0, 2 * Z, look, (jnp.int32(-1),) * (2 * SLOTS))
+    serve(4)
     first_sum(0)
+    project(5)
     serve(1)
     first_sum(1)
     serve(1)
-    project(5)
-    serve(1)
     first_sum(2)
     serve(1)
     first_sum(3)
-    serve(2)
+    serve(1)
     project(6)
+    serve(1)
     first_sum(4)
     second_sum(0)
     serve(1)
+    project_far(0)
     second_sum(1)
-    second_sum(2)
-    serve(1)
-    project_far(0)
     first_sum(5)
-    second_sum(3)
     serve(2)
     project_far(1)
     first_sum(6)
-    second_sum(4)
+    second_sum(2)
     serve(2)
     project_far(2)
+    second_sum(3)
+    second_sum(4)
     second_sum(5)
     assert not coming
 
@@ -386,7 +391,6 @@
 def body(query_nope, query_rope, latent_cache, new_latent, prefix_length, latent_up, out_proj, owners, slot_index):
     nl = new_latent.reshape(16, KVW)
     cache = latent_cache.T
-    smem = pl.BlockSpec(memory_space=pltpu.SMEM)
     hbm = pl.BlockSpec(memory_space=pl.ANY)
     vmem = pl.BlockSpec(memory_space=pltpu.VMEM)
     dma = pltpu.SemaphoreType.DMA
@@ -397,9 +401,12 @@
             pltpu.VMEM((16, 4096), BF16),
             pltpu.VMEM((SLOTS, 8, KVW), BF16),
         ),
-        in_specs=[smem] * 3 + [hbm] * 6,
+        in_specs=[hbm] * 9,
         out_specs=(vmem, vmem),
         scratch_shapes=[
+            pltpu.SMEM((1,), jnp.int32),
+            pltpu.SMEM((64,), jnp.int32),
+            pltpu.SMEM((64,), jnp.int32),
             pltpu.VMEM((SPAN, 512), BF16),
             pltpu.VMEM((SPAN, 256), BF16),
             pltpu.VMEM((KVW, PREFIX), BF16),
@@ -429,7 +436,7 @@
             pltpu.VMEM((3, 16, 128), BF16),
             pltpu.VMEM((2, 16, 640), BF16),
             pltpu.VMEM((2, 16, 640), BF16),
-            dma((6,)),
+            dma((9,)),
             dma((1,)),
             dma((17, nk)),
             dma((2,)),

time: 57.6 us -> 57.1 us (level)
  no operation moved by 1% of the time
where the time goes in v5:
time: 57.1 us; the launch traced here: 56.9 us
  Pallas kernels  54.4 us (95%)
  between operations  1.29 us (2%)
  local copies, waits for them, and re-layouts  1.27 us (2%)
    pallas_call x1, Pallas kernels, body(): pl.pallas_call(kernel, out_shape=(pltpu.VMEM((16, 4096), BF16), pltpu.VME...  54.4 us
    unnamed x2, local copies, waits for them, and re-layouts  1.27 us

profile of v5, /device:TPU:1, one launch (start us, length us, event | category | flops | bytes accessed | tf_op | source)
XLA Modules:
  0.0 56.9 jit_solution(16235206222598689340)
XLA Ops:
  1.3 54.4 %shard_map.104 = (bf16[16,4096]{1,0:T(8,128)(2,1)S(1)}, bf16[4,8,576]{2,1,0:T(8,128)(2,1)S(1)}) custom-call(s32[1]{0:T(128)S(6)} %copy.15.len_hbm, s32[64]{0:T(128)} %own_hbm.1, s32[64]{0:T(128)} %slot_hbm.1, bf16[256,512]{1,0:T(8,128)(2,1)} %qn_hbm.1, bf16[256,256]{1,0:T(8,128)(2,1)} %qr_hbm.1, bf16[576,2048]{1,0:T(8,128)(2,1)} %bitcast.2, ...), custom_call_target="tpu_custom_call" | custom-call | flops 5000000000 | bytes 6000000 | tf_op jit(solution)/shard_map/pallas_call | solution.py:398
  55.7 0.7 %copy.13 = bf16[16,4096]{1,0:T(8,128)(2,1)} copy(bf16[16,4096]{1,0:T(8,128)(2,1)S(1)} %get-tuple-element.2) | data formatting | bytes 262144
  56.3 0.6 %copy.14 = bf16[4,8,576]{2,1,0:T(8,128)(2,1)} copy(bf16[4,8,576]{2,1,0:T(8,128)(2,1)S(1)} %get-tuple-element.3) | data formatting | bytes 73728

commit v6 on v5

--- a/solution.py
+++ b/solution.py
@@ -178,9 +178,9 @@
         k = jnp.concatenate([kv[h * 256 : h * 256 + NOPE], ropes[h % 2]], axis=0)
         pair = h // 2
         q = jnp.concatenate([qn[:, h * 128 : (h + 1) * 128], qr[:, pair * 128 : (pair + 1) * 128]], axis=1)
-        s = jnp.dot((q.astype(F32) * to_bits).astype(BF16), k, preferred_element_type=F32)
+        s = jnp.dot(q, k, preferred_element_type=F32)
         s = jnp.concatenate([s[:, :PREFIX] + old_bias, s[:, PREFIX:] + new_bias], axis=1)
-        return jnp.exp2(s - jnp.max(s, axis=1, keepdims=True)).astype(BF16)
+        return jnp.exp2((s - jnp.max(s, axis=1, keepdims=True)) * to_bits).astype(BF16)
 
     def attend(h, e):
         v = jnp.concatenate([kv[h * 256 + NOPE : (h + 1) * 256], ones], axis=0)
@@ -359,16 +359,15 @@
     swap_dec = remote(dec, dec_in, dec_sem.at[0], dec_sem.at[1], sibling)
     swap_dec.start()
     mine = [pick(codes[s]) for s in range(SLOTS)]
-    swap_dec.wait_recv()
-    for s in range(SLOTS):
-        other = dec_in[s // 2].astype(F32)[(s % 2) * 8 : (s % 2) * 8 + 8]
-        dec_ref[s] = (mine[s] + other)[:, :KVW].astype(BF16)
-
     for s in range(6):
         collect(s)
     direct_sum(0)
     direct_sum(1)
     second_sum(6)
+    swap_dec.wait_recv()
+    for s in range(SLOTS):
+        other = dec_in[s // 2].astype(F32)[(s % 2) * 8 : (s % 2) * 8 + 8]
+        dec_ref[s] = (mine[s] + other)[:, :KVW].astype(BF16)
     collect_far(0)
     collect_far(1)
     collect(6)

time: 57.1 us -> 57.1 us (level)
  no operation moved by 1% of the time
where the time goes in v6:
time: 57.1 us; the launch traced here: 56.9 us
  Pallas kernels  54.4 us (95%)
  between operations  1.29 us (2%)
  local copies, waits for them, and re-layouts  1.27 us (2%)
    pallas_call x1, Pallas kernels, body(): pl.pallas_call(kernel, out_shape=(pltpu.VMEM((16, 4096), BF16), pltpu.VME...  54.4 us
    unnamed x2, local copies, waits for them, and re-layouts  1.27 us

profile of v6, /device:TPU:1, one launch (start us, length us, event | category | flops | bytes accessed | tf_op | source)
XLA Modules:
  0.0 56.9 jit_solution(16222979872640199537)
XLA Ops:
  1.3 54.4 %shard_map.104 = (bf16[16,4096]{1,0:T(8,128)(2,1)S(1)}, bf16[4,8,576]{2,1,0:T(8,128)(2,1)S(1)}) custom-call(s32[1]{0:T(128)S(6)} %copy.15.len_hbm, s32[64]{0:T(128)} %own_hbm.1, s32[64]{0:T(128)} %slot_hbm.1, bf16[256,512]{1,0:T(8,128)(2,1)} %qn_hbm.1, bf16[256,256]{1,0:T(8,128)(2,1)} %qr_hbm.1, bf16[576,2048]{1,0:T(8,128)(2,1)} %bitcast.2, ...), custom_call_target="tpu_custom_call" | custom-call | flops 5000000000 | bytes 6000000 | tf_op jit(solution)/shard_map/pallas_call | solution.py:397
  55.7 0.7 %copy.13 = bf16[16,4096]{1,0:T(8,128)(2,1)} copy(bf16[16,4096]{1,0:T(8,128)(2,1)S(1)} %get-tuple-element.2) | data formatting | bytes 262144
  56.3 0.6 %copy.14 = bf16[4,8,576]{2,1,0:T(8,128)(2,1)} copy(bf16[4,8,576]{2,1,0:T(8,128)(2,1)S(1)} %get-tuple-element.3) | data formatting | bytes 73728
